TPU v7x, 512 devices: a whole 4x4x16 slice. The times are simulated.
512 devices in a mesh: ctx: 16 (over z), batch: 8 (over y, core), mp: 4 (over x).
Axes of the slice: x: 4, y: 4, z: 16, core: 2. Of those that a mesh axis runs over, the one named last changes fastest.
Arguments:
- kv_cache: bfloat16 [2, 16, 16384, 4, 128], P(None, 'batch', 'ctx', 'mp'), may hold values from -6 to 6
- backup_codes: bfloat16 [2, 16, 16384, 4, 128], P(None, 'batch', 'ctx', 'mp'), may hold values from -6 to 6
- backup_scales: bfloat16 [2, 16, 128, 4], P(None, 'batch', 'ctx', 'mp'), may hold values from 0.5 to 2
- block_shift: int32 [8], replicated, may hold values from 1 to 15, as said below
- failed: int32 [1], replicated, may hold values from 0 to 511
- new_lengths: int32 [16, 15], P('batch'), may hold values from 960 to 1216, as said below
- queries: bfloat16 [16, 4, 64, 128], P('batch', None, 'mp'), may hold values from -32 to 32
- new_kv: bfloat16 [2, 16, 4, 4, 128], P(None, 'batch', None, 'mp'), may hold values from -5 to 5
Outputs:
- new_cache: bfloat16 [2, 16, 19456, 4, 128], P(None, 'batch', 'ctx', 'mp')
- attended: bfloat16 [16, 4, 64, 128], P('batch', None, 'mp')
- log_total: float32 [16, 4, 64], P('batch', None, 'mp')
Inputs may be any that keep to these rules, and one draw needn't show every extreme that they name: `new_lengths`: for every sequence the 15 lengths sum to 16384; new shard j begins at or after j * 1024 and ends at or before (j + 2) * 1024; every sequence has a shard of exactly 1216 positions. `block_shift`: some block is held at distance 1, another at distance 16 - 1, another at half the ctx length.
All inputs are finite; a program needn't handle non-finite values.
Results may differ from a plain program's by a relative error of at most 0.0079.
Values may be sent and summed in bfloat16 or wider, within the bound.
A program may use at most 64 MiB of HBM per device.

v0:
```python
import math

import jax
import jax.numpy as jnp
from jax import lax
from jax.sharding import PartitionSpec as P

BLK = 128


far_below = -1e30


def shifted(value, axis, steps):
    count = lax.axis_size(axis)
    pairs = [(source, (source + steps) % count) for source in range(count)]
    return lax.ppermute(value, axis, pairs)


def shifted_2(block, axis, distance):
    devices = range(lax.axis_size(axis))
    route = [(i - distance, i) for i in devices if i - distance in devices]
    return lax.ppermute(block, axis, route)


def merged_2(array, axis, combine):
    everything = jax.tree.map(lambda part: lax.all_gather(part, axis), array)
    initial = jax.tree.map(lambda part: part[0], everything)

    def lap(k, so_far):
        return combine(so_far, jax.tree.map(lambda part: part[k], everything))

    return lax.fori_loop(1, lax.axis_size(axis), lap, initial)


def parity_sign(left_ids, right_ids, bit_count):
    shared = jnp.bitwise_and(left_ids[:, None], right_ids[None, :])
    ones_count = jnp.zeros(shared.shape, jnp.int32)
    for bit_pos in range(bit_count):
        ones_count = ones_count + jnp.bitwise_and(jnp.right_shift(shared, bit_pos), 1)
    return (1 - 2 * (ones_count % 2)).astype(jnp.float32)


def merge_parts(first, second):
    high_first, total_first, mix_first = first
    high_second, total_second, mix_second = second
    highest = jnp.maximum(high_first, high_second)
    factor_first = jnp.exp(high_first - highest)
    factor_second = jnp.exp(high_second - highest)
    totals = total_first * factor_first + total_second * factor_second
    mixture = mix_first * factor_first[..., None] + mix_second * factor_second[..., None]
    return (highest, totals, mixture)


def body(kv_cache, backup_codes, backup_scales, block_shift, failed, new_lengths, queries, new_kv):
    ctx_count = lax.axis_size("ctx")
    mp_count = lax.axis_size("mp")
    ctx_here = lax.axis_index("ctx")
    mp_here = lax.axis_index("mp")
    kv_pairs, seqs_here, ctx_len, heads_here, head_width = kv_cache.shape
    block_count = ctx_len // BLK
    failed_ctx = failed[0] % ctx_count
    owner_mask = (ctx_here - block_shift) % ctx_count == failed_ctx
    blocked = backup_codes.reshape(kv_pairs, seqs_here, block_count, BLK, heads_here, head_width)
    codes_term = jnp.where(
        owner_mask[None, None, :, None, None, None], blocked, jnp.zeros((), jnp.bfloat16)
    ).reshape(backup_codes.shape)
    scales_term = jnp.where(
        owner_mask[None, None, :, None], backup_scales, jnp.zeros((), jnp.bfloat16)
    )
    codes_sum, scales_sum = (
        lax.psum(codes_term, "ctx").astype(jnp.float32),
        lax.psum(scales_term, "ctx").astype(jnp.float32),
    )
    lost_codes, lost_scales = shifted(
        (codes_sum.astype(jnp.bfloat16), scales_sum.astype(jnp.bfloat16)), "batch", -1
    )
    width_ids = jnp.arange(head_width, dtype=jnp.int32)
    hd_sign = parity_sign(width_ids, width_ids, head_width.bit_length()).astype(jnp.bfloat16)
    total_heads = heads_here * mp_count
    my_heads = mp_here * heads_here + jnp.arange(heads_here, dtype=jnp.int32)
    scaling = 1.0 / math.sqrt(total_heads * head_width)
    portion_codes = lax.all_gather(lost_codes, "mp", axis=3, tiled=True)
    portion_scales = lax.all_gather(lost_scales, "mp", axis=3, tiled=True)
    piece_heads = portion_codes.shape[3]
    turned = jnp.einsum(
        "abtkd,de->abtke", portion_codes, hd_sign, preferred_element_type=jnp.float32
    )
    turned = turned.reshape(kv_pairs, seqs_here, block_count, BLK, piece_heads, head_width)
    turned = turned * portion_scales.astype(jnp.float32)[:, :, :, None, :, None]
    their_heads = jnp.arange(piece_heads, dtype=jnp.int32)
    coefs = parity_sign(their_heads, my_heads, total_heads.bit_length()) * scaling
    mixed = jnp.sum(turned[:, :, :, :, :, None, :] * coefs[:, :, None], axis=4)
    restored = mixed.reshape(jnp.zeros(kv_cache.shape, jnp.float32).shape).astype(jnp.bfloat16)
    effective = jnp.where(ctx_here == failed_ctx, restored, kv_cache)
    lower_rows = shifted_2(effective, "ctx", 1)
    extended = jnp.concatenate([lower_rows, effective], axis=2)
    gap_rows = ctx_len // ctx_count
    capacity = ctx_len + 3 * gap_rows
    shard_rank = ctx_here - 1
    is_alive = ctx_here != 0
    begins = jnp.cumsum(new_lengths, axis=1) - new_lengths
    chosen = jnp.arange(new_lengths.shape[1], dtype=jnp.int32) == shard_rank
    my_begin = jnp.sum(jnp.where(chosen[None, :], begins, 0), axis=1)
    my_length = jnp.sum(jnp.where(chosen[None, :], new_lengths, 0), axis=1)
    slot_ids = jnp.arange(capacity, dtype=jnp.int32)
    usable = (slot_ids[None, :] < my_length[:, None]) & is_alive
    row_ids = jnp.clip(
        my_begin[:, None] - (ctx_here - 1) * ctx_len + slot_ids[None, :], 0, 2 * ctx_len - 1
    )
    taken = jax.vmap(
        lambda cache_rows, picked_rows: jnp.take(cache_rows, picked_rows, axis=1),
        in_axes=(1, 0),
        out_axes=1,
    )(extended, row_ids)
    new_cache = jnp.where(usable[None, :, :, None, None], taken, jnp.zeros((), jnp.bfloat16))
    step_count = queries.shape[1]
    group_size = queries.shape[2] // heads_here
    grouped = queries.reshape(seqs_here, step_count, heads_here, group_size, head_width)
    score_scale = 1.0 / math.sqrt(head_width)
    scores = (
        jnp.einsum("stkgd,spkd->sktgp", grouped, new_cache[0], preferred_element_type=jnp.float32)
        * score_scale
    )
    keep_rows = usable[:, None, None, None, :]
    masked = jnp.where(keep_rows, scores, far_below)
    highest = jnp.max(masked, axis=-1)
    weights = jnp.where(keep_rows, jnp.exp(masked - highest[..., None]), 0.0)
    totals = jnp.sum(weights, axis=-1)
    mixture = jnp.einsum(
        "sktgp,spkd->sktgd",
        weights.astype(jnp.bfloat16),
        new_cache[1],
        preferred_element_type=jnp.float32,
    )
    highest, totals, mixture = (highest, totals, mixture)
    merged = merged_2((highest, totals, mixture), "ctx", merge_parts)
    step_ids = jnp.arange(step_count, dtype=jnp.int32)
    causal = (step_ids[None, :] <= step_ids[:, None])[None, None, :, None, :]
    fresh_scores = (
        jnp.einsum("stkgd,sukd->sktgu", grouped, new_kv[0], preferred_element_type=jnp.float32)
        * score_scale
    )
    fresh_masked = jnp.where(causal, fresh_scores, far_below)
    fresh_high = jnp.max(fresh_masked, axis=-1)
    fresh_weights = jnp.where(causal, jnp.exp(fresh_masked - fresh_high[..., None]), 0.0)
    fresh_total = jnp.sum(fresh_weights, axis=-1)
    fresh_mix = jnp.einsum(
        "sktgu,sukd->sktgd",
        fresh_weights.astype(jnp.bfloat16),
        new_kv[1],
        preferred_element_type=jnp.float32,
    )
    final_high, final_total, final_mix = merge_parts(merged, (fresh_high, fresh_total, fresh_mix))
    attended = (final_mix / final_total[..., None]).transpose(0, 2, 1, 3, 4)
    attended = attended.reshape(seqs_here, step_count, heads_here * group_size, head_width).astype(
        jnp.bfloat16
    )
    log_total = (
        (final_high + jnp.log(final_total))
        .transpose(0, 2, 1, 3)
        .reshape(seqs_here, step_count, heads_here * group_size)
    )
    return (new_cache, attended, log_total)


def solution(mesh):
    return jax.shard_map(
        body,
        mesh=mesh,
        in_specs=(
            P(None, "batch", "ctx", "mp", None),
            P(None, "batch", "ctx", "mp", None),
            P(None, "batch", "ctx", "mp"),
            P(),
            P(),
            P("batch", None),
            P("batch", None, "mp", None),
            P(None, "batch", None, "mp", None),
        ),
        out_specs=(
            P(None, "batch", "ctx", "mp", None),
            P("batch", None, "mp", None),
            P("batch", None, "mp"),
        ),
        check_vma=False,
    )
```

profile of v0, /device:TPU:6, one launch (start us, length us, event | category | flops | bytes accessed | tf_op | source)
XLA Modules:
  0.0 378.8 jit_solution(16584381761364169421)
XLA Ops:
  8.6 2.4 broadcast_select_fusion.1
  11.1 143.4 %all-reduce.2.cloned.1.call-done = bf16[2,2,1024,1,128]{4,2,3,1,0:T(8,128)(2,1)} async-done(((bf16[2,2,1024,1,128]{4,2,3,1,0:T(8,128)(2,1)}), bf16[2,2,1024,1,128]{4,2,3,1,0:T(8,128)(2,1)}) %all-reduce.2.cloned.1.call-update) | async-done | bytes 1048592 | tf_op jit(solution)/shard_map/psum | solution.py:72
  154.5 12.6 %collective-permute-done = bf16[2,2,1024,1,128]{4,2,3,1,0:T(8,128)(2,1)S(1)} collective-permute-done((bf16[2,2,1024,1,128]{4,2,3,1,0:T(8,128)(2,1)}, bf16[2,2,1024,1,128]{4,2,3,1,0:T(8,128)(2,1)S(1)}, u32[]{:S(2)}, u32[]{:S(2)}) %collective-permute-start) | collective-permute-done | bytes 1048608 | tf_op jit(solution)/shard_map/ppermute | solution.py:17
  167.1 1.0 copy-done.2
  168.2 29.3 %psum.15 = bf16[2,2,8,1]{2,1,3,0:T(2,128)(2,1)S(1)} all-reduce(bf16[2,2,8,1]{2,1,3,0:T(2,128)(2,1)S(1)} %broadcast_select_fusion.2), channel_id=1, replica_groups=mesh['ctx'=16,'batch'=8,'mp'=4] {'ctx'}, use_global_device_ids=true, to_apply=%region_4.5 | all-reduce | flops 32 | bytes 128 | tf_op jit(solution)/shard_map/psum | solution.py:73
  198.8 6.7 %all_gather.25 = bf16[2,2,8,4]{2,1,3,0:T(2,128)(2,1)S(1)} all-gather(bf16[2,2,8,1]{2,1,3,0:T(2,128)(2,1)S(1)} %collective-permute-done.1), channel_id=1, replica_groups=mesh['ctx'=16,'batch'=8,'mp'=4] {'mp'}, dimensions={3}, use_global_device_ids=true | all-gather | bytes 320 | tf_op jit(solution)/shard_map/all_gather | solution.py:84
  205.6 14.3 %all-gather.6.cloned.1.call-done = bf16[2,2,1024,4,128]{4,2,3,1,0:T(8,128)(2,1)} async-done(((bf16[2,2,1024,1,128]{4,2,3,1,0:T(8,128)(2,1)}), bf16[2,2,1024,4,128]{4,2,3,1,0:T(8,128)(2,1)}) %all-gather.6.cloned.1.call-update) | async-done | bytes 4194320 | tf_op jit(solution)/shard_map/all_gather | solution.py:83
  220.0 5.5 %multiply_reduce_fusion = bf16[2,2,1024,128]{3,2,1,0:T(8,128)(2,1)S(1)} fusion(f32[4]{0:T(128)S(1)} %fusion.54, f32[2,2,1024,4]{2,3,1,0:T(4,128)S(1)} %mul.175, bf16[2,2,1024,4,128]{4,2,3,1,0:T(8,128)(2,1)} %all-gather.6.cloned.1.call-done), kind=kOutput, calls=%fused_computation.11 | convolution fusion | flops 543277056 | bytes 5308432 | tf_op jit(solution)/shard_map/abtkd,de->abtke/dot_general | solution.py:86
  225.4 1.8 broadcast_select_fusion
  227.3 4.7 %collective-permute-start.2 = (bf16[2,2,1024,1,128]{4,0,2,1,3:T(2,128)(2,1)S(1)}, bf16[2,2,1024,1,128]{4,0,2,1,3:T(2,128)(2,1)}, u32[]{:S(2)}, u32[]{:S(2)}) collective-permute-start(bf16[2,2,1024,1,128]{4,0,2,1,3:T(2,128)(2,1)S(1)} %broadcast_select_fusion), channel_id=1, source_target_pairs={{0,32},{32,64},{64,96},{96,128},{128,160},{160,192},{192,224},{224... | collective-permute-start | bytes 3145736 | tf_op jit(solution)/shard_map/ppermute | solution.py:23
  232.3 21.1 %collective-permute-done.2 = bf16[2,2,1024,1,128]{4,0,2,1,3:T(2,128)(2,1)} collective-permute-done((bf16[2,2,1024,1,128]{4,0,2,1,3:T(2,128)(2,1)S(1)}, bf16[2,2,1024,1,128]{4,0,2,1,3:T(2,128)(2,1)}, u32[]{:S(2)}, u32[]{:S(2)}) %collective-permute-start.2) | collective-permute-done | bytes 1048608 | tf_op jit(solution)/shard_map/ppermute | solution.py:23
  253.4 11.9 %maximum_bitcast_fusion = bf16[2,2,2048,128]{3,1,2,0:T(2,128)(2,1)S(1)} fusion(bf16[2,2,1024,1,128]{4,0,2,1,3:T(2,128)(2,1)S(1)} %broadcast_select_fusion, bf16[2,2,1024,1,128]{4,0,2,1,3:T(2,128)(2,1)} %collective-permute-done.2), kind=kLoop, calls=%fused_computation.15 | loop fusion | flops 1048576 | bytes 4194304 | tf_op jit(solution)/shard_map/vmap(jit(_take))/transpose | solution.py:112
  265.3 9.8 %gather_fusion = bf16[2432,2,128]{2,1,0:T(2,128)(2,1)S(1)} fusion(bf16[2,2,2048,128]{3,1,2,0:T(2,128)(2,1)S(1)} %maximum_bitcast_fusion, s32[2432]{0:T(1024)S(1)} %reshape.326), kind=kCustom, calls=%fused_computation | custom fusion | bytes 2509824 | tf_op jit(solution)/shard_map/vmap(jit(_take))/gather | solution.py:112
  275.3 2.2 fusion.14
  279.2 31.6 %all-gather = f32[32,4,16]{2,1,0:T(4,128)S(1)} all-gather(f32[2,4,16]{2,1,0:T(4,128)S(1)} %get-tuple-element.240), channel_id=2, replica_groups=mesh['ctx'=16,'batch'=8,'mp'=4] {'ctx'}, dimensions={0}, use_global_device_ids=true | all-gather | bytes 8704 | tf_op jit(solution)/shard_map/all_gather | solution.py:27
  311.1 28.5 %all-gather.1 = f32[32,4,16]{2,1,0:T(4,128)S(1)} all-gather(f32[2,4,16]{2,1,0:T(4,128)S(1)} %fusion.17), channel_id=3, replica_groups=mesh['ctx'=16,'batch'=8,'mp'=4] {'ctx'}, dimensions={0}, use_global_device_ids=true | all-gather | bytes 8704 | tf_op jit(solution)/shard_map/all_gather | solution.py:27
  339.5 14.8 %all-gather.8.cloned.1.call-done = f32[32,4,16,128]{3,2,1,0:T(8,128)} async-done(((f32[2,4,16,128]{3,2,1,0:T(8,128)}), f32[32,4,16,128]{3,2,1,0:T(8,128)}) %all-gather.8.cloned.1.call-update) | async-done | bytes 1048592 | tf_op jit(solution)/shard_map/all_gather | solution.py:27
  355.2 15.6 %while.19 = (s32[]{:T(128)}, f32[2,1,4,16]{3,2,0,1:T(4,128)S(1)}, f32[2,1,4,16]{3,2,0,1:T(4,128)S(1)}, f32[2,1,4,16,128]{4,3,2,1,0:T(8,128)S(1)}, f32[16,2,1,4,1...) while((s32[]{:T(128)}, f32[2,1,4,16]{3,2,0,1:T(4,128)S(1)}, ...), condition=%wide.region_9.10_spmd, body=%wide.region_8.9_spmd.sunk | while | flops 50053 | bytes 204443 | solution.py:33
  355.2 1.0 fusion.78
  356.3 1.0 fusion.78
  357.3 1.0 fusion.78
  358.3 1.0 fusion.78
  359.4 1.0 fusion.78
  360.4 1.0 fusion.78
  (101 shorter events, 16.3 us)
Async XLA Ops:
  7.2 270.3 %copy-start = (bf16[2,4,16,128]{3,2,1,0:T(8,128)(2,1)S(1)}, bf16[2,4,16,128]{3,2,1,0:T(8,128)(2,1)}, u32[]{:S(2)}) copy-start(bf16[2,4,16,128]{3,2,1,0:T(8,128)(2,1)} %param.16) | copy-start | bytes 98308
  7.2 147.3 %all-reduce.2.cloned.1.call-start = ((), (), s32[]{:S(2)}) async-start(), calls=%async_computation | async-start | bytes 2097152 | tf_op jit(solution)/shard_map/psum | solution.py:72
  11.0 157.1 %copy-start.4 = (bf16[2,2,8,1]{2,1,3,0:T(2,128)(2,1)S(1)}, bf16[2,2,8,1]{2,1,3,0:T(2,128)(2,1)}, u32[]{:S(2)}) copy-start(bf16[2,2,8,1]{2,1,3,0:T(2,128)(2,1)} %param.12) | copy-start | bytes 196
  11.0 186.5 %copy-start.3 = (s32[2,15]{1,0:T(2,128)S(1)}, s32[2,15]{1,0:T(2,128)}, u32[]{:S(2)}) copy-start(s32[2,15]{1,0:T(2,128)} %param.15) | copy-start | bytes 364
  11.1 208.9 %all-gather.6.cloned.1.call-start = ((), (), s32[]{:S(2)}) async-start(), calls=%async_computation.1 | async-start | bytes 5242880 | tf_op jit(solution)/shard_map/all_gather | solution.py:83
  154.5 12.6 %collective-permute-start = (bf16[2,2,1024,1,128]{4,2,3,1,0:T(8,128)(2,1)}, bf16[2,2,1024,1,128]{4,2,3,1,0:T(8,128)(2,1)S(1)}, u32[]{:S(2)}, u32[]{:S(2)}) collective-permute-start(bf16[2,2,1024,1,128]{4,2,3,1,0:T(8,128)(2,1)} %all-reduce.2.cloned.1.call-done), channel_id=1, source_target_pairs={{0,28},{4,0},{8,4},{12,8},{16,12},{20,16},{24,20},{28,24},{1,29},{... | collective-permute-start | bytes 3145736 | tf_op jit(solution)/shard_map/ppermute | solution.py:17
  167.1 1.0 copy-start.2
  168.1 186.2 %all-gather.8.cloned.1.call-start = ((), (), s32[]{:S(2)}) async-start(), calls=%async_computation.2 | async-start | bytes 1114112 | tf_op jit(solution)/shard_map/all_gather | solution.py:27
  197.5 1.3 collective-permute-start.1
  205.6 19.8 %copy-start.1 = (bf16[2,2,1024,1,128]{4,2,3,1,0:T(8,128)(2,1)S(1)}, bf16[2,2,1024,1,128]{4,2,3,1,0:T(8,128)(2,1)}, u32[]{:S(2)}) copy-start(bf16[2,2,1024,1,128]{4,2,3,1,0:T(8,128)(2,1)} %param.10) | copy-start | bytes 3145732
  227.3 26.1 %collective-permute-start.2 = (bf16[2,2,1024,1,128]{4,0,2,1,3:T(2,128)(2,1)S(1)}, bf16[2,2,1024,1,128]{4,0,2,1,3:T(2,128)(2,1)}, u32[]{:S(2)}, u32[]{:S(2)}) collective-permute-start(bf16[2,2,1024,1,128]{4,0,2,1,3:T(2,128)(2,1)S(1)} %broadcast_select_fusion), channel_id=1, source_target_pairs={{0,32},{32,64},{64,96},{96,128},{128,160},{160,192},{192,224},{224... | collective-permute-start | bytes 3145736 | tf_op jit(solution)/shard_map/ppermute | solution.py:23
  277.5 1.4 copy-start.5
Sparse Core Ops, SparseCore 0:
  11.2 143.2 all-reduce.1
  168.3 51.6 all-gather.5
  279.0 75.2 all-gather.7
where the time goes:
time: 380 us; the launch traced here: 379 us
  waiting for transfers between devices  207 us (54%)
  blocking collectives  96 us (25%)
  other arithmetic  35.6 us (9%)
  between operations  14.6 us (4%)
  local copies, waits for them, and re-layouts  12.1 us (3%)
  matrix products  7.96 us (2%)
  starting transfers between devices  4.82 us (1%)
    psum x1, waiting for transfers between devices, body(): lax.psum(codes_term, 'ctx').astype(jnp.float32)  143 us
    all_gather x2, blocking collectives, merged_2(): everything = jax.tree.map(lambda part: lax.all_gather(part, axis), array)  60 us
    psum x1, blocking collectives, body(): lax.psum(scales_term, 'ctx').astype(jnp.float32)  29.3 us
    ppermute x1, waiting for transfers between devices, shifted_2(): return lax.ppermute(block, axis, route)  21.1 us
    all_gather x1, waiting for transfers between devices, merged_2(): everything = jax.tree.map(lambda part: lax.all_gather(part, axis), array)  14.8 us
    add x15, other arithmetic, merge_parts(): mix_first * factor_first[..., None] + mix_second * factor_second[..., None]  14.3 us
    all_gather x1, waiting for transfers between devices, body(): portion_codes = lax.all_gather(lost_codes, 'mp', axis=3, tiled=True)  14.3 us
    ppermute x2, waiting for transfers between devices, shifted(): return lax.ppermute(value, axis, pairs)  13.5 us
  transfers between devices with their start and end apart: 6, of which 6 were waited for; matrix products, arithmetic and copies ran while one was open for 0% of the time, Pallas kernels for 0%

commit v1 on v0

v1 whole, which is shorter than its diff:
```python
import functools
import math

import jax
import jax.numpy as jnp
from jax import lax
from jax.experimental import pallas as pl
from jax.experimental.pallas import tpu as pltpu
from jax.sharding import PartitionSpec as P

F32 = jnp.float32
BF16 = jnp.bfloat16
MESH = pl.DeviceIdType.MESH

far_below = -1e30

BLK = 128
N = 16
NB = 8
MP = 4
HD = 128
CTX = 1024
CAP = 1216
PIECE = CTX // N
ROWS = 2 * PIECE
PACK = ROWS + 16
PART = HD + 16

RS_LEFT, RS_RIGHT = 8, 7
AG_LEFT, AG_RIGHT = 8, 7
PART_LEFT, PART_RIGHT = 9, 6
A_PARTS = 16


def dot_tt(a, b):
    return lax.dot_general(a, b, (((1,), (1,)), ((), ())), preferred_element_type=F32)


def dot_sum_rows(a, b):
    return lax.dot_general(a, b, (((0,), (0,)), ((), ())), preferred_element_type=F32)


def iota(shape, dim):
    return lax.broadcasted_iota(jnp.int32, shape, dim)


def split_three(x):
    hi = x.astype(BF16).astype(F32)
    rest = x - hi
    mid = rest.astype(BF16).astype(F32)
    return hi, mid, rest - mid


def kernel(kv_hbm, codes_hbm, scales_hbm, shift_hbm, failed_hbm, lengths_hbm, q_hbm, fresh_hbm,
           out, att, logs,
           kv, codes, scales, shift, failed, lengths, q, fresh,
           lower, scale_tiles, lbuf, rbuf, xbuf, msgs, parts, qpad, score, own_mix, lost_mix, ext,
           in_sem, a_send, a_recv, l_send, l_recv, r_send, r_recv, x_send, x_recv,
           gl_send, gl_recv, gr_send, gr_recv, pl_send, pl_recv, pr_send, pr_recv):
    z = lax.axis_index("ctx")
    g = lax.axis_index("batch")
    k = lax.axis_index("mp")

    fetch = [
        pltpu.make_async_copy(source, target, in_sem.at[n])
        for n, (source, target) in enumerate((
            (codes_hbm, codes), (failed_hbm, failed), (shift_hbm, shift), (scales_hbm, scales),
            (kv_hbm, kv), (q_hbm, q), (fresh_hbm, fresh), (lengths_hbm, lengths)))
    ]
    for copy in fetch:
        copy.start()

    def ring(c):
        return lax.rem(c + 2 * N, N)

    up, down = ring(z + 1), ring(z - 1)
    g_to, g_from = lax.rem(g + NB - 1, NB), lax.rem(g + 1, NB)

    barrier = pltpu.get_barrier_semaphore()
    for c in (up, down):
        pl.semaphore_signal(barrier, inc=1, device_id=(c, g, k), device_id_type=MESH)
    for j in range(MP):
        pl.semaphore_signal(barrier, inc=1, device_id=(z, g_to, j), device_id_type=MESH)
        pl.semaphore_signal(barrier, inc=1, device_id=(z, g_from, j), device_id_type=MESH)

    for copy in fetch[:4]:
        copy.wait()
    fc = lax.rem(failed[0], N)
    lane = iota((16, HD), 1)
    row = iota((16, HD), 0)

    for p in range(2):
        both = scales[p].astype(F32)
        for b in range(CTX // BLK):
            tile = jnp.where(row == 0, both[0:1, b:b + 1], jnp.where(row == 1, both[1:2, b:b + 1], 0.0))
            scale_tiles[b, p] = tile.astype(BF16)

    def mine(d):
        return lax.rem(fc + shift[d // 2], N) == z

    def select(d, buf, t, p, first):
        start = pl.multiple_of(d * PIECE, PIECE)
        own = mine(d)
        for s in range(2):
            rows = slice(s * PIECE, (s + 1) * PIECE)
            here = codes[2 * p + s, pl.ds(start, PIECE), :]
            buf[t, p, rows, :] = here if first else jnp.where(own, here, buf[t, p, rows, :])
        here = scale_tiles[d // 2, p]
        buf[t, p, ROWS:, :] = here if first else jnp.where(own, here, buf[t, p, ROWS:, :])

    def rs_copy(buf, t, p, target, send, recv):
        return pltpu.make_async_remote_copy(
            src_ref=buf.at[t, p], dst_ref=buf.at[t + 1, p], send_sem=send.at[t, p], recv_sem=recv.at[t, p],
            device_id=(target, g, k), device_id_type=MESH)

    def l_copy(t, p):
        return rs_copy(lbuf, t, p, down, l_send, l_recv)

    def r_copy(t, p):
        return rs_copy(rbuf, t, p, up, r_send, r_recv)

    def ag_copy(t, p, target, source, send, recv):
        return pltpu.make_async_remote_copy(
            src_ref=msgs.at[source, p], dst_ref=msgs.at[source, p], send_sem=send.at[t, p], recv_sem=recv.at[t, p],
            device_id=(target, g, k), device_id_type=MESH)

    def gl_copy(t, p):
        return ag_copy(t, p, down, ring(z + t), gl_send, gl_recv)

    def gl_arrival(t, p):
        return ag_copy(t, p, down, ring(z + t + 1), gl_send, gl_recv)

    def gr_copy(t, p):
        return ag_copy(t, p, up, ring(z - t), gr_send, gr_recv)

    def gr_arrival(t, p):
        return ag_copy(t, p, up, ring(z - t - 1), gr_send, gr_recv)

    def part_copy(t, target, source, send, recv):
        return pltpu.make_async_remote_copy(
            src_ref=parts.at[source], dst_ref=parts.at[source], send_sem=send.at[t], recv_sem=recv.at[t],
            device_id=(target, g, k), device_id_type=MESH)

    def a_copy(n):
        rows = slice(n * (CTX // A_PARTS), (n + 1) * (CTX // A_PARTS))
        return pltpu.make_async_remote_copy(
            src_ref=kv.at[:, rows, :], dst_ref=lower.at[:, rows, :], send_sem=a_send.at[n], recv_sem=a_recv.at[n],
            device_id=(up, g, k), device_id_type=MESH)

    a_started = [0]

    def a_step(count=1):
        first = a_started[0]
        last = min(first + count, A_PARTS)
        a_started[0] = last

        @pl.when(z != N - 1)
        def _():
            for n in range(first, last):
                a_copy(n).start()

    part_step_at = [0]

    def part_step():
        t = part_step_at[0]
        part_step_at[0] = t + 1
        if t < PART_LEFT:
            if t > 0:
                part_copy(t - 1, down, ring(z + t), pl_send, pl_recv).wait_recv()
            part_copy(t, down, ring(z + t), pl_send, pl_recv).start()
        if t < PART_RIGHT:
            if t > 0:
                part_copy(t - 1, up, ring(z - t), pr_send, pr_recv).wait_recv()
            part_copy(t, up, ring(z - t), pr_send, pr_recv).start()

    for p in range(2):
        select(ring(z - RS_LEFT), lbuf, 0, p, True)
        select(ring(z + RS_RIGHT), rbuf, 0, p, True)
    pl.semaphore_wait(barrier, 2 + 2 * MP)
    for p in range(2):
        l_copy(0, p).start()
        r_copy(0, p).start()
    for copy in fetch[4:]:
        copy.wait()
    a_step()

    half = iota((HD, HD), 0) < HD // 2
    queries = q[...]
    zero = jnp.zeros((HD, HD), BF16)
    qpad[0] = jnp.where(half, queries, zero)
    qpad[1] = jnp.where(half, zero, queries)
    first_half = iota((1, HD), 1) < HD // 2
    scaling = 1.0 / math.sqrt(HD)
    alive = z != fc
    CH = 256

    def scores_of(k0, k1):
        return (dot_tt(k0, qpad[0]) + dot_tt(k1, qpad[1])) * scaling

    def weigh(s, top, v0, v1):
        w = jnp.exp(s - top)
        total = jnp.sum(w, axis=0, keepdims=True)
        w0 = jnp.where(first_half, w, 0.0).astype(BF16)
        w1 = jnp.where(first_half, 0.0, w).astype(BF16)
        return total, dot_sum_rows(v0, w0) + dot_sum_rows(v1, w1)

    own = {"top": jnp.full((1, HD), far_below, F32), "total": jnp.zeros((1, HD), F32)}

    def score_part(n):
        rows = slice(n * CH, (n + 1) * CH)
        s = scores_of(kv[0, rows, :], kv[1, rows, :])
        s = jnp.where(alive, s, far_below)
        score[rows, :] = s
        own["top"] = jnp.maximum(own["top"], jnp.max(s, axis=0, keepdims=True))

    def weigh_part(n):
        rows = slice(n * CH, (n + 1) * CH)
        total, mix = weigh(score[rows, :], own["top"], kv[2, rows, :], kv[3, rows, :])
        own["total"] = own["total"] + total
        own_mix[...] = mix if n == 0 else own_mix[...] + mix

    def own_done():
        parts[z, :HD, :] = jnp.where(alive, own_mix[...], 0.0).astype(BF16)
        tile = jnp.zeros((16, HD), F32)
        total = jnp.where(alive, own["total"], 0.0)
        for n, piece in enumerate(split_three(own["top"]) + split_three(total)):
            tile = jnp.where(row == n, piece, tile)
        parts[z, HD:, :] = tile.astype(BF16)
        part_step()

    fresh_part = {}

    def fresh_keys():
        fresh_rows = fresh[...]
        s = dot_tt(fresh_rows, queries) * scaling
        usable = (row < 8) & (row // 4 == lane // 64) & (lax.rem(row, 4) <= lax.rem(lane, 64) // 16)
        s = jnp.where(usable, s, far_below)
        top = jnp.max(s, axis=0, keepdims=True)
        w = jnp.where(usable, jnp.exp(s - top), 0.0)
        fresh_part["total"] = jnp.sum(w, axis=0, keepdims=True)
        fresh_part["top"] = top
        w = jnp.concatenate([jnp.zeros((8, HD), F32), w[:8]], axis=0).astype(BF16)
        fresh_part["mix"] = dot_sum_rows(fresh_rows, w)

    work = {0: [lambda n=n: score_part(n) for n in range(4)],
            1: [lambda n=n: weigh_part(n) for n in range(2)],
            2: [lambda n=n: weigh_part(n) for n in range(2, 4)] + [own_done],
            3: [part_step], 4: [part_step], 5: [part_step], 6: [part_step], 7: [part_step]}

    for thunk in work[0]:
        thunk()
    for t in range(1, max(RS_LEFT, RS_RIGHT)):
        for p in range(2):
            if t < RS_LEFT:
                l_copy(t - 1, p).wait_recv()
                select(ring(z - RS_LEFT + t), lbuf, t, p, False)
                l_copy(t, p).start()
            if t < RS_RIGHT:
                r_copy(t - 1, p).wait_recv()
                select(ring(z + RS_RIGHT - t), rbuf, t, p, False)
                r_copy(t, p).start()
        a_step()
        for thunk in work.get(t, []):
            thunk()

    def x_copy(j, p, slot):
        return pltpu.make_async_remote_copy(
            src_ref=lbuf.at[RS_LEFT, p], dst_ref=xbuf.at[p, slot],
            send_sem=x_send.at[j, p], recv_sem=x_recv.at[slot, p],
            device_id=(z, g_to, j), device_id_type=MESH)

    from_right = ring(lax.rem(fc + shift[z // 2], N) - z) <= RS_LEFT
    for p in range(2):
        r_copy(RS_RIGHT - 1, p).wait_recv()
        l_copy(RS_LEFT - 1, p).wait_recv()
        lbuf[RS_LEFT, p] = jnp.where(from_right, lbuf[RS_LEFT, p], rbuf[RS_RIGHT, p])
        select(z, lbuf, RS_LEFT, p, False)
        for j in range(MP):
            x_copy(j, p, k).start()
    a_step(2)
    part_step()
    fresh_keys()

    shared = iota((HD, HD), 0) & iota((HD, HD), 1)
    shared = shared ^ (shared >> 4)
    shared = shared ^ (shared >> 2)
    shared = (shared ^ (shared >> 1)) & 1
    signs = (1 - 2 * shared).astype(F32).astype(BF16)

    norm = 1.0 / math.sqrt(MP * HD)
    for p in range(2):
        mixed = [None] * 2
        for j in range(MP):
            x_copy(j, p, j).wait_recv()
            common = k & j
            odd = (common ^ (common >> 1)) & 1
            coef = jnp.where(odd == 1, -norm, norm).astype(F32)
            scale_rows = xbuf[p, j, ROWS:, :].astype(F32)
            turned = jnp.dot(xbuf[p, j, :ROWS, :], signs, preferred_element_type=F32)
            for s in range(2):
                term = turned[s * PIECE:(s + 1) * PIECE] * scale_rows[s:s + 1, :] * coef
                mixed[s] = term if j == 0 else mixed[s] + term
        for s in range(2):
            msgs[z, p, s * PIECE:(s + 1) * PIECE, :] = mixed[s].astype(BF16)
        gl_copy(0, p).start()
        gr_copy(0, p).start()

    lost = {}

    def lost_pieces(pieces):
        keys = [jnp.concatenate([msgs[c, 0, s * PIECE:(s + 1) * PIECE, :] for c in pieces], axis=0) for s in range(2)]
        values = [jnp.concatenate([msgs[c, 1, s * PIECE:(s + 1) * PIECE, :] for c in pieces], axis=0) for s in range(2)]
        s = scores_of(*keys)
        top = jnp.max(s, axis=0, keepdims=True)
        if lost:
            top = jnp.maximum(top, lost["top"])
        total, mix = weigh(s, top, *values)
        if lost:
            factor = jnp.exp(lost["top"] - top)
            total = total + lost["total"] * factor
            mix = mix + lost_mix[...] * factor
        lost_mix[...] = mix
        lost["top"], lost["total"] = top, total
        for c in pieces:
            rows = pl.ds(pl.multiple_of(c * PIECE, PIECE), PIECE)
            target = pl.ds(pl.multiple_of(CTX + c * PIECE, PIECE), PIECE)
            for i in range(4):
                rebuilt = msgs[c, i // 2, (i % 2) * PIECE:(i % 2 + 1) * PIECE, :]
                ext[i, target, :] = jnp.where(z == fc, rebuilt, kv[i, rows, :]).astype(F32)

    lost_pieces([z])
    a_step()
    part_step()
    steps = max(AG_LEFT, AG_RIGHT)
    for t in range(1, steps + 1):
        arrived = []
        for p in range(2):
            if t <= AG_LEFT:
                gl_arrival(t - 1, p).wait_recv()
                if t < AG_LEFT:
                    gl_copy(t, p).start()
            if t <= AG_RIGHT:
                gr_arrival(t - 1, p).wait_recv()
                if t < AG_RIGHT:
                    gr_copy(t, p).start()
        if t <= AG_LEFT:
            arrived.append(ring(z + t))
        if t <= AG_RIGHT:
            arrived.append(ring(z - t))
        a_step()
        part_step()
        lost_pieces(arrived)
    a_step(A_PARTS)
    while part_step_at[0] < max(PART_LEFT, PART_RIGHT):
        part_step()
    part_copy(PART_LEFT - 1, down, ring(z + PART_LEFT), pl_send, pl_recv).wait_recv()
    part_copy(PART_RIGHT - 1, up, ring(z - PART_RIGHT), pr_send, pr_recv).wait_recv()

    tops, totals = [fresh_part["top"], lost["top"]], [fresh_part["total"], lost["total"]]
    for c in range(N):
        tile = parts[c, HD:, :].astype(F32)
        tops.append(tile[0:1] + tile[1:2] + tile[2:3])
        totals.append(tile[3:4] + tile[4:5] + tile[5:6])
    top = functools.reduce(jnp.maximum, tops)
    factors = [jnp.exp(v - top) for v in tops]
    total = functools.reduce(jnp.add, [v * f for v, f in zip(totals, factors)])
    mix = fresh_part["mix"] * factors[0] + lost_mix[...] * factors[1]
    for c in range(N):
        mix = mix + parts[c, :HD, :].astype(F32) * factors[c + 2]
    att[...] = jnp.transpose(mix / total).astype(BF16)
    log_row = top + jnp.log(total)
    for n in range(8):
        turned = log_row if n == 0 else pltpu.roll(log_row, HD - 16 * n, 1)
        logs[n // 4, n % 4:n % 4 + 1, :] = turned[:, :16]

    @pl.when(z != 0)
    def _():
        for n in range(A_PARTS):
            a_copy(n).wait_recv()

    for c in range(N):
        rows = slice(c * PIECE, (c + 1) * PIECE)
        for i in range(4):
            rebuilt = msgs[c, i // 2, (i % 2) * PIECE:(i % 2 + 1) * PIECE, :]
            ext[i, rows, :] = jnp.where(z - 1 == fc, rebuilt, lower[i, rows, :]).astype(F32)
    for i in range(4):
        ext[i, 2 * CTX:, :] = jnp.zeros((CAP - CTX, HD), F32)
    for seq in range(2):
        begin = jnp.int32(0)
        length = jnp.int32(0)
        for j in range(N - 1):
            size = lengths[seq, j]
            begin = begin + jnp.where(j < z - 1, size, 0)
            length = jnp.where(j == z - 1, size, length)
        offset = jnp.clip(begin - (z - 1) * CTX, 0, CTX)
        slot = iota((PIECE, HD), 0)
        for p in range(2):
            for n in range(CAP // PIECE):
                rows = ext[2 * p + seq, pl.ds(offset + n * PIECE, PIECE), :]
                rows = jnp.where(slot + n * PIECE < length, rows, 0.0)
                out[2 * p + seq, n * PIECE:(n + 1) * PIECE, :] = rows.astype(BF16)

    for p in range(2):
        for t in range(RS_LEFT):
            l_copy(t, p).wait_send()
        for t in range(RS_RIGHT):
            r_copy(t, p).wait_send()
        for j in range(MP):
            x_copy(j, p, k).wait_send()
        for t in range(AG_LEFT):
            gl_copy(t, p).wait_send()
        for t in range(AG_RIGHT):
            gr_copy(t, p).wait_send()
    for t in range(PART_LEFT):
        part_copy(t, down, ring(z + t), pl_send, pl_recv).wait_send()
    for t in range(PART_RIGHT):
        part_copy(t, up, ring(z - t), pr_send, pr_recv).wait_send()

    @pl.when(z != N - 1)
    def _():
        for n in range(A_PARTS):
            a_copy(n).wait_send()


def body(kv_cache, backup_codes, backup_scales, block_shift, failed, new_lengths, queries, new_kv):
    vmem = pl.BlockSpec(memory_space=pltpu.VMEM)
    hbm = pl.BlockSpec(memory_space=pltpu.HBM)
    dma = pltpu.SemaphoreType.DMA
    out, att, logs = pl.pallas_call(
        kernel,
        out_shape=(
            jax.ShapeDtypeStruct((4, CAP, HD), BF16),
            jax.ShapeDtypeStruct((HD, HD), BF16),
            jax.ShapeDtypeStruct((2, 4, 16), F32),
        ),
        in_specs=[hbm] * 8,
        out_specs=(vmem, vmem, vmem),
        scratch_shapes=[
            pltpu.VMEM((4, CTX, HD), BF16),
            pltpu.VMEM((4, CTX, HD), BF16),
            pltpu.VMEM((2, 2, CTX // BLK), BF16),
            pltpu.SMEM((CTX // BLK,), jnp.int32),
            pltpu.SMEM((1,), jnp.int32),
            pltpu.SMEM((2, N - 1), jnp.int32),
            pltpu.VMEM((HD, HD), BF16),
            pltpu.VMEM((16, HD), BF16),
            pltpu.VMEM((4, CTX, HD), BF16),
            pltpu.VMEM((CTX // BLK, 2, 16, HD), BF16),
            pltpu.VMEM((RS_LEFT + 1, 2, PACK, HD), BF16),
            pltpu.VMEM((RS_RIGHT + 1, 2, PACK, HD), BF16),
            pltpu.VMEM((2, MP, PACK, HD), BF16),
            pltpu.VMEM((N, 2, ROWS, HD), BF16),
            pltpu.VMEM((N, PART, HD), BF16),
            pltpu.VMEM((2, HD, HD), BF16),
            pltpu.VMEM((CTX, HD), F32),
            pltpu.VMEM((HD, HD), F32),
            pltpu.VMEM((HD, HD), F32),
            pltpu.VMEM((4, CTX + CAP, HD), F32),
            dma((8,)),
            dma((A_PARTS,)), dma((A_PARTS,)),
            dma((RS_LEFT, 2)), dma((RS_LEFT, 2)),
            dma((RS_RIGHT, 2)), dma((RS_RIGHT, 2)),
            dma((MP, 2)), dma((MP, 2)),
            dma((AG_LEFT, 2)), dma((AG_LEFT, 2)),
            dma((AG_RIGHT, 2)), dma((AG_RIGHT, 2)),
            dma((PART_LEFT,)), dma((PART_LEFT,)),
            dma((PART_RIGHT,)), dma((PART_RIGHT,)),
        ],
        compiler_params=pltpu.CompilerParams(
            collective_id=0, has_side_effects=True, vmem_limit_bytes=56 * 1024 * 1024),
        cost_estimate=pl.CostEstimate(flops=10**8, bytes_accessed=4 * 10**6, transcendentals=2 * 10**5),
    )(
        kv_cache.reshape(4, CTX, HD),
        backup_codes.reshape(4, CTX, HD),
        backup_scales.reshape(2, 2, CTX // BLK),
        block_shift,
        failed,
        new_lengths,
        queries.reshape(HD, HD),
        new_kv.reshape(16, HD),
    )
    return (
        out.reshape(2, 2, CAP, 1, HD),
        att.reshape(queries.shape),
        logs,
    )


def solution(mesh):
    return jax.shard_map(
        body,
        mesh=mesh,
        in_specs=(
            P(None, "batch", "ctx", "mp", None),
            P(None, "batch", "ctx", "mp", None),
            P(None, "batch", "ctx", "mp"),
            P(),
            P(),
            P("batch", None),
            P("batch", None, "mp", None),
            P(None, "batch", None, "mp", None),
        ),
        out_specs=(
            P(None, "batch", "ctx", "mp", None),
            P("batch", None, "mp", None),
            P("batch", None, "mp"),
        ),
        check_vma=False,
    )
```

time: 380 us -> 79.6 us (0.21)
  the two profiles are of different devices: /device:TPU:6 before, /device:TPU:14 now
where the time goes in v1:
time: 79.6 us; the launch traced here: 79.4 us
  Pallas kernels  74.5 us (94%)
  local copies, waits for them, and re-layouts  3.62 us (5%)
  between operations  1.3 us (2%)
    pallas_call x1, Pallas kernels, body(): pl.pallas_call(kernel, out_shape=(jax.ShapeDtypeStruct((4, CAP, HD), BF16...  74.5 us
    unnamed x7, local copies, waits for them, and re-layouts  3.62 us

profile of v1, /device:TPU:14, one launch (start us, length us, event | category | flops | bytes accessed | tf_op | source)
XLA Modules:
  0.0 79.4 jit_solution(15297327071256219400)
XLA Ops:
  1.3 74.5 %shard_map.103 = (bf16[4,1216,128]{2,1,0:T(8,128)(2,1)}, bf16[128,128]{1,0:T(8,128)(2,1)}, f32[2,4,16]{2,1,0:T(4,128)}) custom-call(bf16[4,1024,128]{2,1,0:T(8,128)(2,1)} %bitcast.10, bf16[4,1024,128]{2,1,0:T(8,128)(2,1)} %bitcast.11, bf16[2,2,8]{2,1,0:T(2,128)(2,1)} %bitcast.15, s32[8]{0:T(128)} %shift_hbm.1, s32[1]{0:T(128)S(6)} %copy.15.failed_hbm, ...), custom_call_target="tpu_custom_call" | custom-call | flops 100000000 | bytes 4000000 | tf_op jit(solution)/shard_map/pallas_call | solution.py:429
  75.8 0.0 copy-start
  75.8 0.0 copy-start.1
  75.8 2.4 %copy.16 = bf16[2,2,1216,1,128]{4,2,3,1,0:T(8,128)(2,1)} copy(bf16[2,2,1216,1,128]{4,2,3,1,0:T(8,128)(2,1)} %bitcast.9) | data formatting | bytes 2490368
  78.2 0.0 copy-done
  78.2 0.6 copy.17
  78.8 0.0 copy-done.1
  78.9 0.6 copy.18
Async XLA Ops:
  75.8 2.4 %copy-start = (bf16[128,128]{1,0:T(8,128)(2,1)S(1)}, bf16[128,128]{1,0:T(8,128)(2,1)}, u32[]{:S(2)}) copy-start(bf16[128,128]{1,0:T(8,128)(2,1)} %get-tuple-element.7) | copy-start | bytes 98308
  75.8 3.0 %copy-start.1 = (f32[2,4,16]{2,1,0:T(4,128)S(1)}, f32[2,4,16]{2,1,0:T(4,128)}, u32[]{:S(2)}) copy-start(f32[2,4,16]{2,1,0:T(4,128)} %get-tuple-element.17) | copy-start | bytes 1540

commit v2 on v1

--- a/solution.py
+++ b/solution.py
@@ -26,9 +26,9 @@
 PACK = ROWS + 16
 PART = HD + 16
 
-RS_LEFT, RS_RIGHT = 8, 7
-AG_LEFT, AG_RIGHT = 8, 7
-PART_LEFT, PART_RIGHT = 9, 6
+RS_LEFT, RS_RIGHT = 10, 5
+AG_LEFT, AG_RIGHT = 10, 5
+PART_LEFT, PART_RIGHT = 15, 0
 A_PARTS = 16
 
 
@@ -245,7 +245,7 @@
     work = {0: [lambda n=n: score_part(n) for n in range(4)],
             1: [lambda n=n: weigh_part(n) for n in range(2)],
             2: [lambda n=n: weigh_part(n) for n in range(2, 4)] + [own_done],
-            3: [part_step], 4: [part_step], 5: [part_step], 6: [part_step], 7: [part_step]}
+            **{t: [part_step] for t in range(3, RS_LEFT)}}
 
     for thunk in work[0]:
         thunk()
@@ -255,10 +255,10 @@
                 l_copy(t - 1, p).wait_recv()
                 select(ring(z - RS_LEFT + t), lbuf, t, p, False)
                 l_copy(t, p).start()
-            if t < RS_RIGHT:
-                r_copy(t - 1, p).wait_recv()
-                select(ring(z + RS_RIGHT - t), rbuf, t, p, False)
-                r_copy(t, p).start()
+            if t % 2 == 0 and t // 2 < RS_RIGHT:
+                r_copy(t // 2 - 1, p).wait_recv()
+                select(ring(z + RS_RIGHT - t // 2), rbuf, t // 2, p, False)
+                r_copy(t // 2, p).start()
         a_step()
         for thunk in work.get(t, []):
             thunk()
@@ -339,14 +339,14 @@
                 gl_arrival(t - 1, p).wait_recv()
                 if t < AG_LEFT:
                     gl_copy(t, p).start()
-            if t <= AG_RIGHT:
-                gr_arrival(t - 1, p).wait_recv()
-                if t < AG_RIGHT:
-                    gr_copy(t, p).start()
+            if t % 2 == 0 and t // 2 <= AG_RIGHT:
+                gr_arrival(t // 2 - 1, p).wait_recv()
+                if t // 2 < AG_RIGHT:
+                    gr_copy(t // 2, p).start()
         if t <= AG_LEFT:
             arrived.append(ring(z + t))
-        if t <= AG_RIGHT:
-            arrived.append(ring(z - t))
+        if t % 2 == 0 and t // 2 <= AG_RIGHT:
+            arrived.append(ring(z - t // 2))
         a_step()
         part_step()
         lost_pieces(arrived)
@@ -354,7 +354,6 @@
     while part_step_at[0] < max(PART_LEFT, PART_RIGHT):
         part_step()
     part_copy(PART_LEFT - 1, down, ring(z + PART_LEFT), pl_send, pl_recv).wait_recv()
-    part_copy(PART_RIGHT - 1, up, ring(z - PART_RIGHT), pr_send, pr_recv).wait_recv()
 
     tops, totals = [fresh_part["top"], lost["top"]], [fresh_part["total"], lost["total"]]
     for c in range(N):
@@ -420,6 +419,15 @@
     def _():
         for n in range(A_PARTS):
             a_copy(n).wait_send()
+
+
+def hand_over(source, att_source, log_source, out, att, logs, sems):
+    pairs = [(source.at[i], out.at[i]) for i in range(4)] + [(att_source, att), (log_source, logs)]
+    copies = [pltpu.make_async_copy(a, b, sems.at[n]) for n, (a, b) in enumerate(pairs)]
+    for copy in copies:
+        copy.start()
+    for copy in copies:
+        copy.wait()
 
 
 def body(kv_cache, backup_codes, backup_scales, block_shift, failed, new_lengths, queries, new_kv):
@@ -464,7 +472,7 @@
             dma((AG_LEFT, 2)), dma((AG_LEFT, 2)),
             dma((AG_RIGHT, 2)), dma((AG_RIGHT, 2)),
             dma((PART_LEFT,)), dma((PART_LEFT,)),
-            dma((PART_RIGHT,)), dma((PART_RIGHT,)),
+            dma((1,)), dma((1,)),
         ],
         compiler_params=pltpu.CompilerParams(
             collective_id=0, has_side_effects=True, vmem_limit_bytes=56 * 1024 * 1024),
@@ -479,6 +487,18 @@
         queries.reshape(HD, HD),
         new_kv.reshape(16, HD),
     )
+    out, att, logs = pl.pallas_call(
+        hand_over,
+        out_shape=(
+            jax.ShapeDtypeStruct((4, CAP, HD), BF16),
+            jax.ShapeDtypeStruct((HD, HD), BF16),
+            jax.ShapeDtypeStruct((2, 4, 16), F32),
+        ),
+        in_specs=[hbm] * 3,
+        out_specs=(hbm,) * 3,
+        scratch_shapes=[dma((6,))],
+        cost_estimate=pl.CostEstimate(flops=0, bytes_accessed=25 * 10**5, transcendentals=0),
+    )(out, att, logs)
     return (
         out.reshape(2, 2, CAP, 1, HD),
         att.reshape(queries.shape),

time: 79.6 us -> 123 us (1.55)
  the two profiles are of different devices: /device:TPU:14 before, /device:TPU:6 now
where the time goes in v2:
time: 123 us; the launch traced here: 121 us
  Pallas kernels  120 us (98%)
  between operations  1.29 us (1%)
    pallas_call x1, Pallas kernels, body(): pl.pallas_call(kernel, out_shape=(jax.ShapeDtypeStruct((4, CAP, HD), BF16...  80.2 us
    pallas_call x1, Pallas kernels, body(): pl.pallas_call(hand_over, out_shape=(jax.ShapeDtypeStruct((4, CAP, HD), B...  40 us

profile of v2, /device:TPU:6, one launch (start us, length us, event | category | flops | bytes accessed | tf_op | source)
XLA Modules:
  0.0 121.5 jit_solution(7699158671010931884)
XLA Ops:
  1.3 80.2 %shard_map.103 = (bf16[4,1216,128]{2,1,0:T(8,128)(2,1)}, bf16[128,128]{1,0:T(8,128)(2,1)}, f32[2,4,16]{2,1,0:T(4,128)}) custom-call(bf16[4,1024,128]{2,1,0:T(8,128)(2,1)} %bitcast.9, bf16[4,1024,128]{2,1,0:T(8,128)(2,1)} %bitcast.10, bf16[2,2,8]{2,1,0:T(2,128)(2,1)} %bitcast.13, s32[8]{0:T(128)} %shift_hbm.1, s32[1]{0:T(128)S(6)} %copy.12.failed_hbm, ...), custom_call_target="tpu_custom_call" | custom-call | flops 100000000 | bytes 4000000 | tf_op jit(solution)/shard_map/pallas_call | solution.py:437
  81.5 40.0 %shard_map.104 = (bf16[4,1216,128]{2,1,0:T(8,128)(2,1)}, bf16[128,128]{1,0:T(8,128)(2,1)}, f32[2,4,16]{2,1,0:T(4,128)}) custom-call(bf16[4,1216,128]{2,1,0:T(8,128)(2,1)} %get-tuple-element.9.source, bf16[128,128]{1,0:T(8,128)(2,1)} %get-tuple-element.10.att_source, f32[2,4,16]{2,1,0:T(4,128)} %get-tuple-element.11.log_source), custom_call_target="tpu_custom_call" | custom-call | bytes 2500000 | tf_op jit(solution)/shard_map/pallas_call | solution.py:490

commit v3 on v1

v3 whole, which is shorter than its diff:
```python
import functools
import math

import jax
import jax.numpy as jnp
from jax import lax
from jax.experimental import pallas as pl
from jax.experimental.pallas import tpu as pltpu
from jax.sharding import PartitionSpec as P

F32 = jnp.float32
BF16 = jnp.bfloat16
MESH = pl.DeviceIdType.MESH

far_below = -1e30

BLK = 128
N = 16
NB = 8
MP = 4
HD = 128
CTX = 1024
CAP = 1216
PIECE = CTX // N
ROWS = 2 * PIECE
PACK = ROWS + 16
BLOCKS = CTX // BLK
SUB = 8

HOPS = 5
A_PARTS = 16


def dot_tt(a, b):
    return lax.dot_general(a, b, (((1,), (1,)), ((), ())), preferred_element_type=F32)


def dot_sum_rows(a, b):
    return lax.dot_general(a, b, (((0,), (0,)), ((), ())), preferred_element_type=F32)


def iota(shape, dim):
    return lax.broadcasted_iota(jnp.int32, shape, dim)


def kernel(slots, kv_hbm, codes_hbm, scales_hbm, shift_hbm, failed_hbm, lengths_hbm, q_hbm, fresh_hbm,
           out, att, logs,
           kv, codes, scales, shift, failed, lengths, q, fresh,
           lower, bsend, bbuf, srow, xsend, xbuf, msgs, score, own_mix, stats, slices, merged, lost_mix, ext,
           in_sem, a_send, a_recv, b_send, b_recv, s_send, s_recv, x_send, x_recv,
           one_send, one_recv, two_send, two_recv, up_send, up_recv,
           st_send, st_recv, sl_send, sl_recv, me_send, me_recv):
    z = lax.axis_index("ctx")
    g = lax.axis_index("batch")
    k = lax.axis_index("mp")

    fetch = [
        pltpu.make_async_copy(source, target, in_sem.at[n])
        for n, (source, target) in enumerate((
            (codes_hbm, codes), (failed_hbm, failed), (shift_hbm, shift), (scales_hbm, scales),
            (kv_hbm, kv), (q_hbm, q), (fresh_hbm, fresh), (lengths_hbm, lengths)))
    ]
    for copy in fetch:
        copy.start()

    def ring(c):
        return lax.rem(c + 2 * N, N)

    g_to, g_from = lax.rem(g + NB - 1, NB), lax.rem(g + 1, NB)

    barrier = pltpu.get_barrier_semaphore()
    for o in range(1, N):
        pl.semaphore_signal(barrier, inc=1, device_id=(ring(z + o), g, k), device_id_type=MESH)
    for j in range(MP):
        pl.semaphore_signal(barrier, inc=1, device_id=(z, g_to, j), device_id_type=MESH)
        pl.semaphore_signal(barrier, inc=1, device_id=(z, g_from, j), device_id_type=MESH)

    for copy in fetch[:4]:
        copy.wait()
    fc = lax.rem(failed[0], N)
    lane = iota((16, HD), 1)
    row = iota((16, HD), 0)

    shifts = [shift[b] for b in range(BLOCKS)]
    holder = [lax.rem(fc + v, N) for v in shifts]
    rank = []
    for b in range(BLOCKS):
        before = jnp.int32(0)
        for e in range(b):
            before = before + jnp.where(shifts[e] == shifts[b], 1, 0)
        rank.append(jnp.minimum(before, slots - 1))
    def chosen(b, h, j):
        return (holder[b] == h) & (rank[b] == j)

    for j in range(slots):
        for p in range(2):
            pair = []
            for s in range(2):
                block = codes[2 * p + s, j * BLK:(j + 1) * BLK, :]
                for b in range(j + 1, BLOCKS):
                    block = jnp.where(chosen(b, z, j), codes[2 * p + s, b * BLK:(b + 1) * BLK, :], block)
                pair.append(block.astype(F32))
            for c in range(N):
                part = slice(c * SUB, (c + 1) * SUB)
                bsend[c, j, p] = jnp.concatenate([pair[0][part], pair[1][part]], axis=0).astype(BF16)
    line = jnp.zeros((1, HD), F32)
    for p in range(2):
        both = scales[p].astype(F32)
        for s in range(2):
            wide = jnp.concatenate([both[s:s + 1], jnp.zeros((1, HD - BLOCKS), F32)], axis=1)
            at = (2 * p + s) * BLOCKS
            line = line + (pltpu.roll(wide, at, 1) if at else wide)
    srow[z] = line
    bbuf[z] = bsend[z]

    def peer_copy(o, source, target, send, recv):
        return pltpu.make_async_remote_copy(
            src_ref=source, dst_ref=target, send_sem=send.at[o], recv_sem=recv.at[o],
            device_id=(ring(z + o), g, k), device_id_type=MESH)

    def b_copy(o):
        return peer_copy(o, bsend.at[ring(z + o)], bbuf.at[z], b_send, b_recv)

    def s_copy(o):
        return peer_copy(o, srow.at[z], srow.at[z], s_send, s_recv)

    def st_copy(o):
        return peer_copy(o, stats.at[z], stats.at[z], st_send, st_recv)

    def sl_copy(o):
        rows = pl.ds(pl.multiple_of(ring(z + o) * SUB, SUB), SUB)
        return peer_copy(o, own_mix.at[rows, :], slices.at[z], sl_send, sl_recv)

    def me_copy(o):
        return peer_copy(o, merged.at[z], merged.at[z], me_send, me_recv)

    order = [8, 7, 9, 6, 10, 5, 11, 4, 12, 3, 13, 2, 14, 1, 15]
    pl.semaphore_wait(barrier, N - 1 + 2 * MP)
    for o in order:
        b_copy(o).start()
        s_copy(o).start()

    def a_copy(n):
        rows = slice(n * (CTX // A_PARTS), (n + 1) * (CTX // A_PARTS))
        return pltpu.make_async_remote_copy(
            src_ref=kv.at[:, rows, :], dst_ref=lower.at[:, rows, :], send_sem=a_send.at[n], recv_sem=a_recv.at[n],
            device_id=(ring(z + 1), g, k), device_id_type=MESH)

    a_started = [0]

    def a_step(count):
        first = a_started[0]
        last = min(first + count, A_PARTS)
        a_started[0] = last

        @pl.when(z != N - 1)
        def _():
            for n in range(first, last):
                a_copy(n).start()

    for copy in fetch[4:]:
        copy.wait()

    half = iota((HD, HD), 0) < HD // 2
    queries = q[...]
    zero = jnp.zeros((HD, HD), BF16)
    q0, q1 = jnp.where(half, queries, zero), jnp.where(half, zero, queries)
    first_half = iota((1, HD), 1) < HD // 2
    scaling = 1.0 / math.sqrt(HD)
    alive = z != fc
    CH = 256

    top_own = jnp.full((1, HD), far_below, F32)
    for n in range(CTX // CH):
        rows = slice(n * CH, (n + 1) * CH)
        s = (dot_tt(kv[0, rows, :], q0) + dot_tt(kv[1, rows, :], q1)) * scaling
        s = jnp.where(alive, s, far_below)
        score[rows, :] = s
        top_own = jnp.maximum(top_own, jnp.max(s, axis=0, keepdims=True))
    total_own = jnp.zeros((1, HD), F32)
    for n in range(CTX // CH):
        rows = slice(n * CH, (n + 1) * CH)
        w = jnp.where(alive, jnp.exp(score[rows, :] - top_own), 0.0)
        total_own = total_own + jnp.sum(w, axis=0, keepdims=True)
        w0 = jnp.where(first_half, w, 0.0).astype(BF16)
        w1 = jnp.where(first_half, 0.0, w).astype(BF16)
        mix = dot_sum_rows(kv[2, rows, :], w0) + dot_sum_rows(kv[3, rows, :], w1)
        own_mix[...] = mix if n == 0 else own_mix[...] + mix
    stats[z, 0] = top_own
    stats[z, 1] = total_own
    slices[z] = own_mix[pl.ds(pl.multiple_of(z * SUB, SUB), SUB), :]

    fresh_rows = fresh[...]
    s = dot_tt(fresh_rows, queries) * scaling
    usable = (row < 8) & (row // 4 == lane // 64) & (lax.rem(row, 4) <= lax.rem(lane, 64) // 16)
    s = jnp.where(usable, s, far_below)
    top_fresh = jnp.max(s, axis=0, keepdims=True)
    w = jnp.where(usable, jnp.exp(s - top_fresh), 0.0)
    total_fresh = jnp.sum(w, axis=0, keepdims=True)
    w = jnp.concatenate([jnp.zeros((8, HD), F32), w[:8]], axis=0).astype(BF16)
    mix_fresh = dot_sum_rows(fresh_rows, w)

    shared = iota((HD, HD), 0) & iota((HD, HD), 1)
    shared = shared ^ (shared >> 4)
    shared = shared ^ (shared >> 2)
    shared = (shared ^ (shared >> 1)) & 1
    signs = (1 - 2 * shared).astype(F32).astype(BF16)

    for i in range(4):
        for n in range(CTX // CH):
            ext[i, CTX + n * CH:CTX + (n + 1) * CH, :] = kv[i, n * CH:(n + 1) * CH, :].astype(F32)
        ext[i, 2 * CTX:, :] = jnp.zeros((CAP - CTX, HD), F32)

    for o in order:
        b_copy(o).wait_recv()
        s_copy(o).wait_recv()
    tiles = [jnp.zeros((16, HD), F32) for _ in range(2)]
    for b in range(BLOCKS):
        line = srow[0]
        for h in range(1, N):
            line = jnp.where(holder[b] == h, srow[h], line)
        for p in range(2):
            for s in range(2):
                at = (2 * p + s) * BLOCKS + b
                tiles[p] = jnp.where(row == 2 * b + s, line[:, at:at + 1], tiles[p])

    def x_copy(j, p, slot):
        return pltpu.make_async_remote_copy(
            src_ref=xsend.at[p], dst_ref=xbuf.at[p, slot],
            send_sem=x_send.at[j, p], recv_sem=x_recv.at[slot, p],
            device_id=(z, g_to, j), device_id_type=MESH)

    for p in range(2):
        for b in range(BLOCKS):
            tile = bbuf[0, 0, p]
            for h in range(N):
                for j in range(min(slots, b + 1)):
                    if h + j > 0:
                        tile = jnp.where(chosen(b, h, j), bbuf[h, j, p], tile)
            xsend[p, b * 16:(b + 1) * 16, :] = tile
        xsend[p, ROWS:, :] = tiles[p].astype(BF16)
        for j in range(MP):
            x_copy(j, p, k).start()
    for o in order:
        st_copy(o).start()
        sl_copy(o).start()
    a_step(5)

    def one_copy(t, p, piece):
        return pltpu.make_async_remote_copy(
            src_ref=msgs.at[piece, p], dst_ref=msgs.at[piece, p], send_sem=one_send.at[t, p], recv_sem=one_recv.at[t, p],
            device_id=(ring(z - 1), g, k), device_id_type=MESH)

    def two_copy(t, p, piece):
        return pltpu.make_async_remote_copy(
            src_ref=msgs.at[piece, p], dst_ref=msgs.at[piece, p], send_sem=two_send.at[t, p], recv_sem=two_recv.at[t, p],
            device_id=(ring(z - 2), g, k), device_id_type=MESH)

    def up_copy(t, p, piece):
        return pltpu.make_async_remote_copy(
            src_ref=msgs.at[piece, p], dst_ref=msgs.at[piece, p], send_sem=up_send.at[t, p], recv_sem=up_recv.at[t, p],
            device_id=(ring(z + 1), g, k), device_id_type=MESH)

    norm = 1.0 / math.sqrt(MP * HD)
    for p in range(2):
        mixed = None
        for j in range(MP):
            x_copy(j, p, j).wait_recv()
            common = k & j
            odd = (common ^ (common >> 1)) & 1
            coef = jnp.where(odd == 1, -norm, norm).astype(F32)
            tile = xbuf[p, j, ROWS:, :].astype(F32)
            wide = jnp.concatenate([jnp.broadcast_to(tile[r:r + 1], (SUB, HD)) for r in range(16)], axis=0)
            term = jnp.dot(xbuf[p, j, :ROWS, :], signs, preferred_element_type=F32) * wide * coef
            mixed = term if j == 0 else mixed + term
        msgs[z, p] = mixed.astype(BF16)
        two_copy(0, p, z).start()
        up_copy(0, p, z).start()
        one_copy(0, p, z).start()

    lost = {}

    def lost_pieces(pieces):
        count = len(pieces)
        keys = jnp.concatenate([msgs[c, 0] for c in pieces], axis=0)
        values = jnp.concatenate([msgs[c, 1] for c in pieces], axis=0)
        matching = ((iota((ROWS * count, HD), 0) // SUB) & 1) == iota((ROWS * count, HD), 1) // (HD // 2)
        s = jnp.where(matching, dot_tt(keys, queries) * scaling, far_below)
        top = jnp.max(s, axis=0, keepdims=True)
        if lost:
            top = jnp.maximum(top, lost["top"])
        w = jnp.where(matching, jnp.exp(s - top), 0.0)
        total = jnp.sum(w, axis=0, keepdims=True)
        mix = dot_sum_rows(values, w.astype(BF16))
        if lost:
            factor = jnp.exp(lost["top"] - top)
            total = total + lost["total"] * factor
            mix = mix + lost_mix[...] * factor
        lost_mix[...] = mix
        lost["top"], lost["total"] = top, total
        for c in pieces:
            for p in range(2):
                for b in range(BLOCKS):
                    tile = msgs[c, p, b * 16:(b + 1) * 16, :].astype(F32)
                    rows = pl.ds(pl.multiple_of(CTX + b * BLK + c * SUB, SUB), SUB)
                    for s in range(2):
                        ext[2 * p + s, rows, :] = jnp.where(
                            z == fc, tile[s * SUB:(s + 1) * SUB], ext[2 * p + s, rows, :])

    a_step(2)
    lost_pieces([z])

    for o in order:
        st_copy(o).wait_recv()
        sl_copy(o).wait_recv()
    tops = [stats[c, 0] for c in range(N)]
    top_alive = functools.reduce(jnp.maximum, tops)
    factors = [jnp.exp(v - top_alive) for v in tops]
    total_alive = functools.reduce(jnp.add, [stats[c, 1] * factors[c] for c in range(N)])
    merged[z] = functools.reduce(jnp.add, [slices[c] * factors[c] for c in range(N)])
    for o in order:
        me_copy(o).start()

    for t in range(1, HOPS + 1):
        for p in range(2):
            two_copy(t - 1, p, ring(z + 2 * t)).wait_recv()
            if t < HOPS:
                two_copy(t, p, ring(z + 2 * t)).start()
                one_copy(t, p, ring(z + 2 * t)).start()
            up_copy(t - 1, p, ring(z - t)).wait_recv()
            if t < HOPS:
                up_copy(t, p, ring(z - t)).start()
        a_step(2)
        for p in range(2):
            one_copy(t - 1, p, ring(z + 2 * t - 1)).wait_recv()
        lost_pieces([ring(z + 2 * t - 1), ring(z + 2 * t), ring(z - t)])
    for o in order:
        me_copy(o).wait_recv()

    tops = [top_fresh, lost["top"], top_alive]
    totals = [total_fresh, lost["total"], total_alive]
    top = functools.reduce(jnp.maximum, tops)
    factors = [jnp.exp(v - top) for v in tops]
    total = functools.reduce(jnp.add, [v * f for v, f in zip(totals, factors)])
    mix = mix_fresh * factors[0] + lost_mix[...] * factors[1]
    mix = mix + jnp.concatenate([merged[c] for c in range(N)], axis=0) * factors[2]
    att[...] = jnp.transpose(mix / total).astype(BF16)
    log_row = top + jnp.log(total)
    for n in range(8):
        turned = log_row if n == 0 else pltpu.roll(log_row, HD - 16 * n, 1)
        logs[n // 4, n % 4:n % 4 + 1, :] = turned[:, :16]

    @pl.when(z != 0)
    def _():
        for n in range(A_PARTS):
            a_copy(n).wait_recv()

    for p in range(2):
        for b in range(BLOCKS):
            tiles = [msgs[c, p, b * 16:(b + 1) * 16, :].astype(F32) for c in range(N)]
            rows = slice(b * BLK, (b + 1) * BLK)
            for s in range(2):
                rebuilt = jnp.concatenate([tile[s * SUB:(s + 1) * SUB] for tile in tiles], axis=0)
                ext[2 * p + s, rows, :] = jnp.where(z - 1 == fc, rebuilt, lower[2 * p + s, rows, :].astype(F32))
    for seq in range(2):
        begin = jnp.int32(0)
        length = jnp.int32(0)
        for j in range(N - 1):
            size = lengths[seq, j]
            begin = begin + jnp.where(j < z - 1, size, 0)
            length = jnp.where(j == z - 1, size, length)
        offset = jnp.clip(begin - (z - 1) * CTX, 0, CTX)
        slot = iota((PIECE, HD), 0)
        for p in range(2):
            for n in range(CAP // PIECE):
                rows = ext[2 * p + seq, pl.ds(offset + n * PIECE, PIECE), :]
                rows = jnp.where(slot + n * PIECE < length, rows, 0.0)
                out[2 * p + seq, n * PIECE:(n + 1) * PIECE, :] = rows.astype(BF16)

    for o in order:
        for make in (b_copy, s_copy, st_copy, sl_copy, me_copy):
            make(o).wait_send()
    for p in range(2):
        for j in range(MP):
            x_copy(j, p, k).wait_send()
        for t in range(HOPS):
            two_copy(t, p, ring(z + 2 * t)).wait_send()
            one_copy(t, p, ring(z + 2 * t)).wait_send()
            up_copy(t, p, ring(z - t)).wait_send()

    @pl.when(z != N - 1)
    def _():
        for n in range(A_PARTS):
            a_copy(n).wait_send()


def restore(slots, *operands):
    vmem = pl.BlockSpec(memory_space=pltpu.VMEM)
    hbm = pl.BlockSpec(memory_space=pltpu.HBM)
    dma = pltpu.SemaphoreType.DMA
    return pl.pallas_call(
        functools.partial(kernel, slots),
        out_shape=(
            jax.ShapeDtypeStruct((4, CAP, HD), BF16),
            jax.ShapeDtypeStruct((HD, HD), BF16),
            jax.ShapeDtypeStruct((2, 4, 16), F32),
        ),
        in_specs=[hbm] * 8,
        out_specs=(vmem, vmem, vmem),
        scratch_shapes=[
            pltpu.VMEM((4, CTX, HD), BF16),
            pltpu.VMEM((4, CTX, HD), BF16),
            pltpu.VMEM((2, 2, BLOCKS), BF16),
            pltpu.SMEM((BLOCKS,), jnp.int32),
            pltpu.SMEM((1,), jnp.int32),
            pltpu.SMEM((2, N - 1), jnp.int32),
            pltpu.VMEM((HD, HD), BF16),
            pltpu.VMEM((16, HD), BF16),
            pltpu.VMEM((4, CTX, HD), BF16),
            pltpu.VMEM((N, slots, 2, 16, HD), BF16),
            pltpu.VMEM((N, slots, 2, 16, HD), BF16),
            pltpu.VMEM((N, 1, HD), F32),
            pltpu.VMEM((2, PACK, HD), BF16),
            pltpu.VMEM((2, MP, PACK, HD), BF16),
            pltpu.VMEM((N, 2, ROWS, HD), BF16),
            pltpu.VMEM((CTX, HD), F32),
            pltpu.VMEM((HD, HD), F32),
            pltpu.VMEM((N, 2, 1, HD), F32),
            pltpu.VMEM((N, SUB, HD), F32),
            pltpu.VMEM((N, SUB, HD), F32),
            pltpu.VMEM((HD, HD), F32),
            pltpu.VMEM((4, CTX + CAP, HD), F32),
            dma((8,)),
            dma((A_PARTS,)), dma((A_PARTS,)),
            dma((N,)), dma((N,)), dma((N,)), dma((N,)),
            dma((MP, 2)), dma((MP, 2)),
            dma((HOPS, 2)), dma((HOPS, 2)),
            dma((HOPS, 2)), dma((HOPS, 2)),
            dma((HOPS, 2)), dma((HOPS, 2)),
            dma((N,)), dma((N,)), dma((N,)), dma((N,)), dma((N,)), dma((N,)),
        ],
        compiler_params=pltpu.CompilerParams(
            collective_id=slots, has_side_effects=True, vmem_limit_bytes=56 * 1024 * 1024),
        cost_estimate=pl.CostEstimate(flops=10**8, bytes_accessed=4 * 10**6, transcendentals=2 * 10**5),
    )(*operands)


SLOTS = (2, 3, 8)


def body(kv_cache, backup_codes, backup_scales, block_shift, failed, new_lengths, queries, new_kv):
    most = jnp.max(jnp.sum((block_shift[:, None] == block_shift[None, :]).astype(jnp.int32), axis=1))
    branch = (most > 2).astype(jnp.int32) + (most > 3).astype(jnp.int32)
    out, att, logs = lax.switch(
        branch,
        [functools.partial(restore, slots) for slots in SLOTS],
        kv_cache.reshape(4, CTX, HD),
        backup_codes.reshape(4, CTX, HD),
        backup_scales.reshape(2, 2, BLOCKS),
        block_shift,
        failed,
        new_lengths,
        queries.reshape(HD, HD),
        new_kv.reshape(16, HD),
    )
    return (
        out.reshape(2, 2, CAP, 1, HD),
        att.reshape(queries.shape),
        logs,
    )


def solution(mesh):
    return jax.shard_map(
        body,
        mesh=mesh,
        in_specs=(
            P(None, "batch", "ctx", "mp", None),
            P(None, "batch", "ctx", "mp", None),
            P(None, "batch", "ctx", "mp"),
            P(),
            P(),
            P("batch", None),
            P("batch", None, "mp", None),
            P(None, "batch", None, "mp", None),
        ),
        out_specs=(
            P(None, "batch", "ctx", "mp", None),
            P("batch", None, "mp", None),
            P("batch", None, "mp"),
        ),
        check_vma=False,
    )
```

time: 79.6 us -> 74.5 us (0.936)
  the two profiles are of different devices: /device:TPU:14 before, /device:TPU:48 now
where the time goes in v3:
time: 74.5 us; the launch traced here: 74.3 us
  Pallas kernels  68.3 us (92%)
  local copies, waits for them, and re-layouts  2.24 us (3%)
  between operations  1.94 us (3%)
  other arithmetic  1.55 us (2%)
    pallas_call x1, Pallas kernels, restore(): pl.pallas_call(functools.partial(kernel, slots), out_shape=(jax.ShapeDtyp...  68.3 us
    unnamed x3, local copies, waits for them, and re-layouts  2.24 us

profile of v3, /device:TPU:48, one launch (start us, length us, event | category | flops | bytes accessed | tf_op | source)
XLA Modules:
  0.0 74.3 jit_solution(6358982832536674521)
XLA Ops:
  0.6 0.9 %convert_reduce_fusion = s32[8]{0:T(128)S(1)} fusion(s32[8]{0:T(128)} %param.14), kind=kLoop, calls=%fused_computation | loop fusion | flops 184 | bytes 64 | tf_op jit(solution)/shard_map/reduce_sum | solution.py:452
  1.5 0.6 reduce_max.9
  3.5 68.5 %conditional.1 = ((bf16[4,1216,128]{2,1,0:T(8,128)(2,1)S(1)}, bf16[128,128]{1,0:T(8,128)(2,1)S(1)}, f32[2,4,16]{2,1,0:T(4,128)S(1)})) conditional(s32[]{:T(128)} %clamp.3, (bf16[4,1024,128]{2,1,0:T(8,128)(2,1)}, bf16[4,1024,128]{2,1,0:T(8,128)(2,1)}, bf16[2,2,8]{2,1,0:T(2,128)(2,1)}, s32[8]{0:T(128)}, s32[1]{0:T(128)}, ...), branch_computations={%region_2.0_spmd, %region_3.0_spmd, %region_4.0_spmd} | conditional | flops 100000000 | bytes 4000008 | solution.py:454
  3.5 68.3 %branch_0_fun.1 = (bf16[4,1216,128]{2,1,0:T(8,128)(2,1)S(1)}, bf16[128,128]{1,0:T(8,128)(2,1)S(1)}, f32[2,4,16]{2,1,0:T(4,128)S(1)}) custom-call(bf16[4,1024,128]{2,1,0:T(8,128)(2,1)} %get-tuple-element.59.kv_hbm, bf16[4,1024,128]{2,1,0:T(8,128)(2,1)} %get-tuple-element.60.codes_hbm, bf16[2,2,8]{2,1,0:T(2,128)(2,1)} %get-tuple-element.61.scales_hbm, ...), custom_call_target="tpu_custom_call" | custom-call | flops 100000000 | bytes 4000000 | tf_op jit(solution)/shard_map/cond/branch_0_fun/pallas_call | solution.py:401
  72.0 1.0 %copy.25 = bf16[2,2,1216,1,128]{4,2,3,1,0:T(8,128)(2,1)} copy(bf16[2,2,1216,1,128]{4,2,3,1,0:T(8,128)(2,1)S(1)} %bitcast.15) | data formatting | bytes 2490368
  73.1 0.6 copy.26
  73.7 0.6 copy.27

commit v4 on v3

--- a/solution.py
+++ b/solution.py
@@ -46,7 +46,7 @@
 def kernel(slots, kv_hbm, codes_hbm, scales_hbm, shift_hbm, failed_hbm, lengths_hbm, q_hbm, fresh_hbm,
            out, att, logs,
            kv, codes, scales, shift, failed, lengths, q, fresh,
-           lower, bsend, bbuf, srow, xsend, xbuf, msgs, score, own_mix, stats, slices, merged, lost_mix, ext,
+           lower, bsend, bbuf, srow, xsend, xbuf, msgs, score, own_mix, sent_mix, stats, slices, merged, lost_mix, ext,
            in_sem, a_send, a_recv, b_send, b_recv, s_send, s_recv, x_send, x_recv,
            one_send, one_recv, two_send, two_recv, up_send, up_recv,
            st_send, st_recv, sl_send, sl_recv, me_send, me_recv):
@@ -127,12 +127,18 @@
     def st_copy(o):
         return peer_copy(o, stats.at[z], stats.at[z], st_send, st_recv)
 
-    def sl_copy(o):
-        rows = pl.ds(pl.multiple_of(ring(z + o) * SUB, SUB), SUB)
-        return peer_copy(o, own_mix.at[rows, :], slices.at[z], sl_send, sl_recv)
-
-    def me_copy(o):
-        return peer_copy(o, merged.at[z], merged.at[z], me_send, me_recv)
+    def sl_copy(i, source):
+        return pltpu.make_async_remote_copy(
+            src_ref=sent_mix.at[i], dst_ref=slices.at[source], send_sem=sl_send.at[i], recv_sem=sl_recv.at[source],
+            device_id=(2 * i, g, k), device_id_type=MESH)
+
+    def me_copy(o, i):
+        return pltpu.make_async_remote_copy(
+            src_ref=merged.at[i], dst_ref=merged.at[i], send_sem=me_send.at[o], recv_sem=me_recv.at[i],
+            device_id=(ring(z + o), g, k), device_id_type=MESH)
+
+    merging = lax.rem(z, 2) == 0
+    my_slice = z // 2
 
     order = [8, 7, 9, 6, 10, 5, 11, 4, 12, 3, 13, 2, 14, 1, 15]
     pl.semaphore_wait(barrier, N - 1 + 2 * MP)
@@ -188,7 +194,9 @@
         own_mix[...] = mix if n == 0 else own_mix[...] + mix
     stats[z, 0] = top_own
     stats[z, 1] = total_own
-    slices[z] = own_mix[pl.ds(pl.multiple_of(z * SUB, SUB), SUB), :]
+    for i in range(N // 2):
+        sent_mix[i] = own_mix[16 * i:16 * i + 16, :].astype(BF16)
+    slices[z] = sent_mix[my_slice]
 
     fresh_rows = fresh[...]
     s = dot_tt(fresh_rows, queries) * scaling
@@ -243,8 +251,11 @@
             x_copy(j, p, k).start()
     for o in order:
         st_copy(o).start()
-        sl_copy(o).start()
-    a_step(5)
+    for i in range(N // 2):
+        @pl.when(z != 2 * i)
+        def _():
+            sl_copy(i, z).start()
+    a_step(7)
 
     def one_copy(t, p, piece):
         return pltpu.make_async_remote_copy(
@@ -302,25 +313,48 @@
             for p in range(2):
                 for b in range(BLOCKS):
                     tile = msgs[c, p, b * 16:(b + 1) * 16, :].astype(F32)
-                    rows = pl.ds(pl.multiple_of(CTX + b * BLK + c * SUB, SUB), SUB)
+                    below = pl.ds(pl.multiple_of(b * BLK + c * SUB, SUB), SUB)
+                    here = pl.ds(pl.multiple_of(CTX + b * BLK + c * SUB, SUB), SUB)
                     for s in range(2):
-                        ext[2 * p + s, rows, :] = jnp.where(
-                            z == fc, tile[s * SUB:(s + 1) * SUB], ext[2 * p + s, rows, :])
-
-    a_step(2)
+                        rebuilt = tile[s * SUB:(s + 1) * SUB]
+                        ext[2 * p + s, here, :] = jnp.where(z == fc, rebuilt, ext[2 * p + s, here, :])
+                        ext[2 * p + s, below, :] = jnp.where(z - 1 == fc, rebuilt, ext[2 * p + s, below, :])
+
+    a_step(3)
     lost_pieces([z])
 
     for o in order:
         st_copy(o).wait_recv()
-        sl_copy(o).wait_recv()
     tops = [stats[c, 0] for c in range(N)]
     top_alive = functools.reduce(jnp.maximum, tops)
     factors = [jnp.exp(v - top_alive) for v in tops]
     total_alive = functools.reduce(jnp.add, [stats[c, 1] * factors[c] for c in range(N)])
-    merged[z] = functools.reduce(jnp.add, [slices[c] * factors[c] for c in range(N)])
-    for o in order:
-        me_copy(o).start()
-
+
+    @pl.when(merging)
+    def _():
+        for c in range(N):
+            @pl.when(z != c)
+            def _():
+                sl_copy(0, c).wait_recv()
+        total_mix = functools.reduce(jnp.add, [slices[c].astype(F32) * factors[c] for c in range(N)])
+        merged[my_slice] = total_mix.astype(BF16)
+        for o in order:
+            me_copy(o, my_slice).start()
+
+    lost_below = z - 1 == fc
+
+    def lower_parts(first, last):
+        @pl.when(z != 0)
+        def _():
+            for n in range(first, last):
+                a_copy(n).wait_recv()
+
+        for n in range(first, last):
+            rows = slice(n * (CTX // A_PARTS), (n + 1) * (CTX // A_PARTS))
+            for i in range(4):
+                ext[i, rows, :] = jnp.where(lost_below, ext[i, rows, :], lower[i, rows, :].astype(F32))
+
+    lower_at = {2: (0, 5), 3: (5, 9), 4: (9, 11), 5: (11, 14)}
     for t in range(1, HOPS + 1):
         for p in range(2):
             two_copy(t - 1, p, ring(z + 2 * t)).wait_recv()
@@ -331,11 +365,15 @@
             if t < HOPS:
                 up_copy(t, p, ring(z - t)).start()
         a_step(2)
+        if t >= 2:
+            lower_parts(*lower_at[t])
         for p in range(2):
             one_copy(t - 1, p, ring(z + 2 * t - 1)).wait_recv()
         lost_pieces([ring(z + 2 * t - 1), ring(z + 2 * t), ring(z - t)])
-    for o in order:
-        me_copy(o).wait_recv()
+    for i in range(N // 2):
+        @pl.when(z != 2 * i)
+        def _():
+            me_copy(1, i).wait_recv()
 
     tops = [top_fresh, lost["top"], top_alive]
     totals = [total_fresh, lost["total"], total_alive]
@@ -343,25 +381,14 @@
     factors = [jnp.exp(v - top) for v in tops]
     total = functools.reduce(jnp.add, [v * f for v, f in zip(totals, factors)])
     mix = mix_fresh * factors[0] + lost_mix[...] * factors[1]
-    mix = mix + jnp.concatenate([merged[c] for c in range(N)], axis=0) * factors[2]
+    mix = mix + jnp.concatenate([merged[i].astype(F32) for i in range(N // 2)], axis=0) * factors[2]
     att[...] = jnp.transpose(mix / total).astype(BF16)
     log_row = top + jnp.log(total)
     for n in range(8):
         turned = log_row if n == 0 else pltpu.roll(log_row, HD - 16 * n, 1)
         logs[n // 4, n % 4:n % 4 + 1, :] = turned[:, :16]
 
-    @pl.when(z != 0)
-    def _():
-        for n in range(A_PARTS):
-            a_copy(n).wait_recv()
-
-    for p in range(2):
-        for b in range(BLOCKS):
-            tiles = [msgs[c, p, b * 16:(b + 1) * 16, :].astype(F32) for c in range(N)]
-            rows = slice(b * BLK, (b + 1) * BLK)
-            for s in range(2):
-                rebuilt = jnp.concatenate([tile[s * SUB:(s + 1) * SUB] for tile in tiles], axis=0)
-                ext[2 * p + s, rows, :] = jnp.where(z - 1 == fc, rebuilt, lower[2 * p + s, rows, :].astype(F32))
+    lower_parts(14, A_PARTS)
     for seq in range(2):
         begin = jnp.int32(0)
         length = jnp.int32(0)
@@ -378,8 +405,18 @@
                 out[2 * p + seq, n * PIECE:(n + 1) * PIECE, :] = rows.astype(BF16)
 
     for o in order:
-        for make in (b_copy, s_copy, st_copy, sl_copy, me_copy):
+        for make in (b_copy, s_copy, st_copy):
             make(o).wait_send()
+    for i in range(N // 2):
+        @pl.when(z != 2 * i)
+        def _():
+            sl_copy(i, z).wait_send()
+
+    @pl.when(merging)
+    def _():
+        for o in order:
+            me_copy(o, my_slice).wait_send()
+
     for p in range(2):
         for j in range(MP):
             x_copy(j, p, k).wait_send()
@@ -425,9 +462,10 @@
             pltpu.VMEM((N, 2, ROWS, HD), BF16),
             pltpu.VMEM((CTX, HD), F32),
             pltpu.VMEM((HD, HD), F32),
+            pltpu.VMEM((N // 2, 16, HD), BF16),
             pltpu.VMEM((N, 2, 1, HD), F32),
-            pltpu.VMEM((N, SUB, HD), F32),
-            pltpu.VMEM((N, SUB, HD), F32),
+            pltpu.VMEM((N, 16, HD), BF16),
+            pltpu.VMEM((N // 2, 16, HD), BF16),
             pltpu.VMEM((HD, HD), F32),
             pltpu.VMEM((4, CTX + CAP, HD), F32),
             dma((8,)),
@@ -449,8 +487,12 @@
 
 
 def body(kv_cache, backup_codes, backup_scales, block_shift, failed, new_lengths, queries, new_kv):
-    most = jnp.max(jnp.sum((block_shift[:, None] == block_shift[None, :]).astype(jnp.int32), axis=1))
-    branch = (most > 2).astype(jnp.int32) + (most > 3).astype(jnp.int32)
+    cube = (BLOCKS,) * 3
+    ids = [lax.broadcasted_iota(jnp.int32, cube, n) for n in range(3)]
+    spread = [lax.broadcast_in_dim(block_shift, cube, (n,)) for n in range(3)]
+    equal = (spread[0] == spread[1]) & (spread[1] == spread[2]) & (ids[0] < ids[1]) & (ids[1] < ids[2])
+    triples = jnp.sum(equal.astype(jnp.int32))
+    branch = (triples > 0).astype(jnp.int32) + (triples > 3).astype(jnp.int32)
     out, att, logs = lax.switch(
         branch,
         [functools.partial(restore, slots) for slots in SLOTS],

time: 74.5 us -> 74.2 us (level)
  the two profiles are of different devices: /device:TPU:48 before, /device:TPU:6 now
where the time goes in v4:
time: 74.2 us; the launch traced here: 73.2 us
  Pallas kernels  67.3 us (91%)
  local copies, waits for them, and re-layouts  2.24 us (3%)
  between operations  1.94 us (3%)
  other arithmetic  1.48 us (2%)
    pallas_call x1, Pallas kernels, restore(): pl.pallas_call(functools.partial(kernel, slots), out_shape=(jax.ShapeDtyp...  67.3 us
    unnamed x3, local copies, waits for them, and re-layouts  2.24 us

profile of v4, /device:TPU:6, one launch (start us, length us, event | category | flops | bytes accessed | tf_op | source)
XLA Modules:
  0.0 73.2 jit_solution(8019366008658542081)
XLA Ops:
  0.6 1.5 %convert_reduce_fusion = s32[]{:T(128)} fusion(s32[8]{0:T(128)} %param.14), kind=kLoop, calls=%fused_computation | loop fusion | flops 4607 | bytes 36 | tf_op jit(solution)/shard_map/reduce_sum | solution.py:494
  3.4 67.6 %conditional.1 = ((bf16[4,1216,128]{2,1,0:T(8,128)(2,1)S(1)}, bf16[128,128]{1,0:T(8,128)(2,1)S(1)}, f32[2,4,16]{2,1,0:T(4,128)S(1)})) conditional(s32[]{:T(128)} %clamp.3, (bf16[4,1024,128]{2,1,0:T(8,128)(2,1)}, bf16[4,1024,128]{2,1,0:T(8,128)(2,1)}, bf16[2,2,8]{2,1,0:T(2,128)(2,1)}, s32[8]{0:T(128)}, s32[1]{0:T(128)}, ...), branch_computations={%region_1.0_spmd, %region_2.0_spmd, %region_3.0_spmd} | conditional | flops 100000000 | bytes 4000008 | solution.py:496
  3.4 67.3 %branch_0_fun.1 = (bf16[4,1216,128]{2,1,0:T(8,128)(2,1)S(1)}, bf16[128,128]{1,0:T(8,128)(2,1)S(1)}, f32[2,4,16]{2,1,0:T(4,128)S(1)}) custom-call(bf16[4,1024,128]{2,1,0:T(8,128)(2,1)} %get-tuple-element.59.kv_hbm, bf16[4,1024,128]{2,1,0:T(8,128)(2,1)} %get-tuple-element.60.codes_hbm, bf16[2,2,8]{2,1,0:T(2,128)(2,1)} %get-tuple-element.61.scales_hbm, ...), custom_call_target="tpu_custom_call" | custom-call | flops 100000000 | bytes 4000000 | tf_op jit(solution)/shard_map/cond/branch_0_fun/pallas_call | solution.py:438
  71.0 1.0 %copy.25 = bf16[2,2,1216,1,128]{4,2,3,1,0:T(8,128)(2,1)} copy(bf16[2,2,1216,1,128]{4,2,3,1,0:T(8,128)(2,1)S(1)} %bitcast.15) | data formatting | bytes 2490368
  72.0 0.6 copy.26
  72.6 0.6 copy.27

commit v5 on v4

--- a/solution.py
+++ b/solution.py
@@ -28,7 +28,7 @@
 SUB = 8
 
 HOPS = 5
-A_PARTS = 16
+A_PARTS = 8
 
 
 def dot_tt(a, b):
@@ -41,15 +41,33 @@
 
 def iota(shape, dim):
     return lax.broadcasted_iota(jnp.int32, shape, dim)
+
+
+def split_three(x):
+    hi = x.astype(BF16).astype(F32)
+    rest = x - hi
+    mid = rest.astype(BF16).astype(F32)
+    return hi, mid, rest - mid
+
+
+def stat_tile(row, top, total):
+    tile = jnp.zeros((16, HD), F32)
+    for n, piece in enumerate(split_three(top) + split_three(total)):
+        tile = jnp.where(row == n, piece, tile)
+    return tile.astype(BF16)
+
+
+def stat_rows(tile):
+    tile = tile.astype(F32)
+    return tile[0:1] + tile[1:2] + tile[2:3], tile[3:4] + tile[4:5] + tile[5:6]
 
 
 def kernel(slots, kv_hbm, codes_hbm, scales_hbm, shift_hbm, failed_hbm, lengths_hbm, q_hbm, fresh_hbm,
            out, att, logs,
            kv, codes, scales, shift, failed, lengths, q, fresh,
-           lower, bsend, bbuf, srow, xsend, xbuf, msgs, score, own_mix, sent_mix, stats, slices, merged, lost_mix, ext,
+           lower, bsend, bbuf, srow, xsend, xbuf, msgs, score, own_mix, sent_mix, slices, merged, all_mix, lost_mix, ext,
            in_sem, a_send, a_recv, b_send, b_recv, s_send, s_recv, x_send, x_recv,
-           one_send, one_recv, two_send, two_recv, up_send, up_recv,
-           st_send, st_recv, sl_send, sl_recv, me_send, me_recv):
+           one_recv, two_recv, up_recv, g_send, sl_send, sl_recv, me_send, me_recv):
     z = lax.axis_index("ctx")
     g = lax.axis_index("batch")
     k = lax.axis_index("mp")
@@ -110,33 +128,30 @@
             wide = jnp.concatenate([both[s:s + 1], jnp.zeros((1, HD - BLOCKS), F32)], axis=1)
             at = (2 * p + s) * BLOCKS
             line = line + (pltpu.roll(wide, at, 1) if at else wide)
-    srow[z] = line
-    bbuf[z] = bsend[z]
+    srow[N - 1] = line
+    bbuf[N - 1] = bsend[z]
 
     def peer_copy(o, source, target, send, recv):
         return pltpu.make_async_remote_copy(
-            src_ref=source, dst_ref=target, send_sem=send.at[o], recv_sem=recv.at[o],
+            src_ref=source, dst_ref=target, send_sem=send, recv_sem=recv,
             device_id=(ring(z + o), g, k), device_id_type=MESH)
 
     def b_copy(o):
-        return peer_copy(o, bsend.at[ring(z + o)], bbuf.at[z], b_send, b_recv)
+        return peer_copy(o, bsend.at[ring(z + o)], bbuf.at[o - 1], b_send, b_recv)
 
     def s_copy(o):
-        return peer_copy(o, srow.at[z], srow.at[z], s_send, s_recv)
-
-    def st_copy(o):
-        return peer_copy(o, stats.at[z], stats.at[z], st_send, st_recv)
-
-    def sl_copy(i, source):
-        return pltpu.make_async_remote_copy(
-            src_ref=sent_mix.at[i], dst_ref=slices.at[source], send_sem=sl_send.at[i], recv_sem=sl_recv.at[source],
-            device_id=(2 * i, g, k), device_id_type=MESH)
-
-    def me_copy(o, i):
-        return pltpu.make_async_remote_copy(
-            src_ref=merged.at[i], dst_ref=merged.at[i], send_sem=me_send.at[o], recv_sem=me_recv.at[i],
-            device_id=(ring(z + o), g, k), device_id_type=MESH)
-
+        return peer_copy(o, srow.at[N - 1], srow.at[o - 1], s_send, s_recv)
+
+    def sl_copy(o):
+        return peer_copy(o, sent_mix.at[ring(z + o) // 2], slices.at[o - 1], sl_send, sl_recv)
+
+    def me_copy(o):
+        return peer_copy(o, merged.at[N // 2 - 1], merged.at[(o - 1) // 2], me_send, me_recv)
+
+    def whole(ref, send, recv):
+        return peer_copy(1, ref, ref, send, recv)
+
+    even, odd = range(2, N, 2), range(1, N, 2)
     merging = lax.rem(z, 2) == 0
     my_slice = z // 2
 
@@ -149,7 +164,7 @@
     def a_copy(n):
         rows = slice(n * (CTX // A_PARTS), (n + 1) * (CTX // A_PARTS))
         return pltpu.make_async_remote_copy(
-            src_ref=kv.at[:, rows, :], dst_ref=lower.at[:, rows, :], send_sem=a_send.at[n], recv_sem=a_recv.at[n],
+            src_ref=kv.at[:, rows, :], dst_ref=lower.at[:, rows, :], send_sem=a_send, recv_sem=a_recv.at[n],
             device_id=(ring(z + 1), g, k), device_id_type=MESH)
 
     a_started = [0]
@@ -192,11 +207,11 @@
         w1 = jnp.where(first_half, 0.0, w).astype(BF16)
         mix = dot_sum_rows(kv[2, rows, :], w0) + dot_sum_rows(kv[3, rows, :], w1)
         own_mix[...] = mix if n == 0 else own_mix[...] + mix
-    stats[z, 0] = top_own
-    stats[z, 1] = total_own
+    tile = stat_tile(row, top_own, total_own)
     for i in range(N // 2):
-        sent_mix[i] = own_mix[16 * i:16 * i + 16, :].astype(BF16)
-    slices[z] = sent_mix[my_slice]
+        sent_mix[i, :16, :] = own_mix[16 * i:16 * i + 16, :].astype(BF16)
+        sent_mix[i, 16:, :] = tile
+    slices[N - 1] = sent_mix[my_slice]
 
     fresh_rows = fresh[...]
     s = dot_tt(fresh_rows, queries) * scaling
@@ -219,14 +234,15 @@
             ext[i, CTX + n * CH:CTX + (n + 1) * CH, :] = kv[i, n * CH:(n + 1) * CH, :].astype(F32)
         ext[i, 2 * CTX:, :] = jnp.zeros((CAP - CTX, HD), F32)
 
-    for o in order:
-        b_copy(o).wait_recv()
-        s_copy(o).wait_recv()
+    whole(bbuf.at[0:N - 1], b_send, b_recv).wait_recv()
+    whole(srow.at[0:N - 1], s_send, s_recv).wait_recv()
+    away = [ring(z - h) for h in holder]
+    away = [jnp.where(v == 0, N - 1, v - 1) for v in away]
     tiles = [jnp.zeros((16, HD), F32) for _ in range(2)]
     for b in range(BLOCKS):
         line = srow[0]
         for h in range(1, N):
-            line = jnp.where(holder[b] == h, srow[h], line)
+            line = jnp.where(away[b] == h, srow[h], line)
         for p in range(2):
             for s in range(2):
                 at = (2 * p + s) * BLOCKS + b
@@ -235,7 +251,7 @@
     def x_copy(j, p, slot):
         return pltpu.make_async_remote_copy(
             src_ref=xsend.at[p], dst_ref=xbuf.at[p, slot],
-            send_sem=x_send.at[j, p], recv_sem=x_recv.at[slot, p],
+            send_sem=x_send.at[p], recv_sem=x_recv.at[p],
             device_id=(z, g_to, j), device_id_type=MESH)
 
     for p in range(2):
@@ -244,39 +260,43 @@
             for h in range(N):
                 for j in range(min(slots, b + 1)):
                     if h + j > 0:
-                        tile = jnp.where(chosen(b, h, j), bbuf[h, j, p], tile)
+                        tile = jnp.where((away[b] == h) & (rank[b] == j), bbuf[h, j, p], tile)
             xsend[p, b * 16:(b + 1) * 16, :] = tile
         xsend[p, ROWS:, :] = tiles[p].astype(BF16)
         for j in range(MP):
             x_copy(j, p, k).start()
-    for o in order:
-        st_copy(o).start()
-    for i in range(N // 2):
-        @pl.when(z != 2 * i)
-        def _():
-            sl_copy(i, z).start()
-    a_step(7)
+    @pl.when(merging)
+    def _():
+        for o in even:
+            sl_copy(o).start()
+
+    @pl.when(jnp.logical_not(merging))
+    def _():
+        for o in odd:
+            sl_copy(o).start()
+
+    a_step(3)
 
     def one_copy(t, p, piece):
         return pltpu.make_async_remote_copy(
-            src_ref=msgs.at[piece, p], dst_ref=msgs.at[piece, p], send_sem=one_send.at[t, p], recv_sem=one_recv.at[t, p],
+            src_ref=msgs.at[piece, p], dst_ref=msgs.at[piece, p], send_sem=g_send, recv_sem=one_recv.at[t, p],
             device_id=(ring(z - 1), g, k), device_id_type=MESH)
 
     def two_copy(t, p, piece):
         return pltpu.make_async_remote_copy(
-            src_ref=msgs.at[piece, p], dst_ref=msgs.at[piece, p], send_sem=two_send.at[t, p], recv_sem=two_recv.at[t, p],
+            src_ref=msgs.at[piece, p], dst_ref=msgs.at[piece, p], send_sem=g_send, recv_sem=two_recv.at[t, p],
             device_id=(ring(z - 2), g, k), device_id_type=MESH)
 
     def up_copy(t, p, piece):
         return pltpu.make_async_remote_copy(
-            src_ref=msgs.at[piece, p], dst_ref=msgs.at[piece, p], send_sem=up_send.at[t, p], recv_sem=up_recv.at[t, p],
+            src_ref=msgs.at[piece, p], dst_ref=msgs.at[piece, p], send_sem=g_send, recv_sem=up_recv.at[t, p],
             device_id=(ring(z + 1), g, k), device_id_type=MESH)
 
     norm = 1.0 / math.sqrt(MP * HD)
     for p in range(2):
         mixed = None
+        whole(xbuf.at[p], x_send.at[p], x_recv.at[p]).wait_recv()
         for j in range(MP):
-            x_copy(j, p, j).wait_recv()
             common = k & j
             odd = (common ^ (common >> 1)) & 1
             coef = jnp.where(odd == 1, -norm, norm).astype(F32)
@@ -320,26 +340,21 @@
                         ext[2 * p + s, here, :] = jnp.where(z == fc, rebuilt, ext[2 * p + s, here, :])
                         ext[2 * p + s, below, :] = jnp.where(z - 1 == fc, rebuilt, ext[2 * p + s, below, :])
 
-    a_step(3)
+    a_step(2)
     lost_pieces([z])
 
-    for o in order:
-        st_copy(o).wait_recv()
-    tops = [stats[c, 0] for c in range(N)]
-    top_alive = functools.reduce(jnp.maximum, tops)
-    factors = [jnp.exp(v - top_alive) for v in tops]
-    total_alive = functools.reduce(jnp.add, [stats[c, 1] * factors[c] for c in range(N)])
-
     @pl.when(merging)
     def _():
-        for c in range(N):
-            @pl.when(z != c)
-            def _():
-                sl_copy(0, c).wait_recv()
-        total_mix = functools.reduce(jnp.add, [slices[c].astype(F32) * factors[c] for c in range(N)])
-        merged[my_slice] = total_mix.astype(BF16)
-        for o in order:
-            me_copy(o, my_slice).start()
+        whole(slices.at[0:N - 1], sl_send, sl_recv).wait_recv()
+        tops, totals = zip(*[stat_rows(slices[c, 16:, :]) for c in range(N)])
+        top = functools.reduce(jnp.maximum, tops)
+        factors = [jnp.exp(v - top) for v in tops]
+        total = functools.reduce(jnp.add, [v * f for v, f in zip(totals, factors)])
+        mix = functools.reduce(jnp.add, [slices[c, :16, :].astype(F32) * factors[c] for c in range(N)])
+        merged[N // 2 - 1, :16, :] = mix.astype(BF16)
+        merged[N // 2 - 1, 16:, :] = stat_tile(row, top, total)
+        for o in range(1, N):
+            me_copy(o).start()
 
     lost_below = z - 1 == fc
 
@@ -354,7 +369,7 @@
             for i in range(4):
                 ext[i, rows, :] = jnp.where(lost_below, ext[i, rows, :], lower[i, rows, :].astype(F32))
 
-    lower_at = {2: (0, 5), 3: (5, 9), 4: (9, 11), 5: (11, 14)}
+    lower_at = {3: (0, 3), 4: (3, 5), 5: (5, 7)}
     for t in range(1, HOPS + 1):
         for p in range(2):
             two_copy(t - 1, p, ring(z + 2 * t)).wait_recv()
@@ -364,16 +379,23 @@
             up_copy(t - 1, p, ring(z - t)).wait_recv()
             if t < HOPS:
                 up_copy(t, p, ring(z - t)).start()
-        a_step(2)
-        if t >= 2:
+        a_step(1)
+        if t in lower_at:
             lower_parts(*lower_at[t])
         for p in range(2):
             one_copy(t - 1, p, ring(z + 2 * t - 1)).wait_recv()
         lost_pieces([ring(z + 2 * t - 1), ring(z + 2 * t), ring(z - t)])
-    for i in range(N // 2):
-        @pl.when(z != 2 * i)
-        def _():
-            me_copy(1, i).wait_recv()
+    @pl.when(merging)
+    def _():
+        whole(merged.at[0:N // 2 - 1], me_send, me_recv).wait_recv()
+
+    @pl.when(jnp.logical_not(merging))
+    def _():
+        whole(merged, me_send, me_recv).wait_recv()
+
+    for n in range(N // 2):
+        all_mix[lax.rem(my_slice + N - n - jnp.where(merging, 1, 0), N // 2)] = merged[n, :16, :].astype(F32)
+    top_alive, total_alive = stat_rows(merged[0, 16:, :])
 
     tops = [top_fresh, lost["top"], top_alive]
     totals = [total_fresh, lost["total"], total_alive]
@@ -381,14 +403,14 @@
     factors = [jnp.exp(v - top) for v in tops]
     total = functools.reduce(jnp.add, [v * f for v, f in zip(totals, factors)])
     mix = mix_fresh * factors[0] + lost_mix[...] * factors[1]
-    mix = mix + jnp.concatenate([merged[i].astype(F32) for i in range(N // 2)], axis=0) * factors[2]
+    mix = mix + jnp.concatenate([all_mix[i] for i in range(N // 2)], axis=0) * factors[2]
     att[...] = jnp.transpose(mix / total).astype(BF16)
     log_row = top + jnp.log(total)
     for n in range(8):
         turned = log_row if n == 0 else pltpu.roll(log_row, HD - 16 * n, 1)
         logs[n // 4, n % 4:n % 4 + 1, :] = turned[:, :16]
 
-    lower_parts(14, A_PARTS)
+    lower_parts(7, A_PARTS)
     for seq in range(2):
         begin = jnp.int32(0)
         length = jnp.int32(0)
@@ -404,31 +426,24 @@
                 rows = jnp.where(slot + n * PIECE < length, rows, 0.0)
                 out[2 * p + seq, n * PIECE:(n + 1) * PIECE, :] = rows.astype(BF16)
 
-    for o in order:
-        for make in (b_copy, s_copy, st_copy):
-            make(o).wait_send()
-    for i in range(N // 2):
-        @pl.when(z != 2 * i)
-        def _():
-            sl_copy(i, z).wait_send()
+    whole(bbuf.at[0:N - 1], b_send, b_recv).wait_send()
+    whole(srow.at[0:N - 1], s_send, s_recv).wait_send()
+    for p in range(2):
+        whole(xbuf.at[p], x_send.at[p], x_recv.at[p]).wait_send()
+    whole(msgs.at[0:N - 1], g_send, up_recv.at[0, 0]).wait_send()
 
     @pl.when(merging)
     def _():
-        for o in order:
-            me_copy(o, my_slice).wait_send()
-
-    for p in range(2):
-        for j in range(MP):
-            x_copy(j, p, k).wait_send()
-        for t in range(HOPS):
-            two_copy(t, p, ring(z + 2 * t)).wait_send()
-            one_copy(t, p, ring(z + 2 * t)).wait_send()
-            up_copy(t, p, ring(z - t)).wait_send()
+        whole(slices.at[0:N // 2 - 1], sl_send, sl_recv).wait_send()
+        whole(slices.at[0:N - 1], me_send, me_recv).wait_send()
+
+    @pl.when(jnp.logical_not(merging))
+    def _():
+        whole(slices.at[0:N // 2], sl_send, sl_recv).wait_send()
 
     @pl.when(z != N - 1)
     def _():
-        for n in range(A_PARTS):
-            a_copy(n).wait_send()
+        whole(lower, a_send, a_recv.at[0]).wait_send()
 
 
 def restore(slots, *operands):
@@ -462,20 +477,18 @@
             pltpu.VMEM((N, 2, ROWS, HD), BF16),
             pltpu.VMEM((CTX, HD), F32),
             pltpu.VMEM((HD, HD), F32),
-            pltpu.VMEM((N // 2, 16, HD), BF16),
-            pltpu.VMEM((N, 2, 1, HD), F32),
-            pltpu.VMEM((N, 16, HD), BF16),
-            pltpu.VMEM((N // 2, 16, HD), BF16),
+            pltpu.VMEM((N // 2, 32, HD), BF16),
+            pltpu.VMEM((N, 32, HD), BF16),
+            pltpu.VMEM((N // 2, 32, HD), BF16),
+            pltpu.VMEM((N // 2, 16, HD), F32),
             pltpu.VMEM((HD, HD), F32),
             pltpu.VMEM((4, CTX + CAP, HD), F32),
             dma((8,)),
-            dma((A_PARTS,)), dma((A_PARTS,)),
-            dma((N,)), dma((N,)), dma((N,)), dma((N,)),
-            dma((MP, 2)), dma((MP, 2)),
-            dma((HOPS, 2)), dma((HOPS, 2)),
-            dma((HOPS, 2)), dma((HOPS, 2)),
-            dma((HOPS, 2)), dma((HOPS, 2)),
-            dma((N,)), dma((N,)), dma((N,)), dma((N,)), dma((N,)), dma((N,)),
+            dma, dma((A_PARTS,)),
+            dma, dma, dma, dma,
+            dma((2,)), dma((2,)),
+            dma((HOPS, 2)), dma((HOPS, 2)), dma((HOPS, 2)),
+            dma, dma, dma, dma, dma,
         ],
         compiler_params=pltpu.CompilerParams(
             collective_id=slots, has_side_effects=True, vmem_limit_bytes=56 * 1024 * 1024),

time: 74.2 us -> 74.6 us (level)
  no operation moved by 1% of the time
where the time goes in v5:
time: 74.6 us; the launch traced here: 73.4 us
  Pallas kernels  67.5 us (90%)
  local copies, waits for them, and re-layouts  2.24 us (3%)
  between operations  1.94 us (3%)
  other arithmetic  1.48 us (2%)
    pallas_call x1, Pallas kernels, restore(): pl.pallas_call(functools.partial(kernel, slots), out_shape=(jax.ShapeDtyp...  67.5 us
    unnamed x3, local copies, waits for them, and re-layouts  2.24 us

profile of v5, /device:TPU:6, one launch (start us, length us, event | category | flops | bytes accessed | tf_op | source)
XLA Modules:
  0.0 73.4 jit_solution(2660059157509690756)
XLA Ops:
  0.6 1.5 %convert_reduce_fusion = s32[]{:T(128)} fusion(s32[8]{0:T(128)} %param.14), kind=kLoop, calls=%fused_computation | loop fusion | flops 4607 | bytes 36 | tf_op jit(solution)/shard_map/reduce_sum | solution.py:507
  3.4 67.8 %conditional.1 = ((bf16[4,1216,128]{2,1,0:T(8,128)(2,1)S(1)}, bf16[128,128]{1,0:T(8,128)(2,1)S(1)}, f32[2,4,16]{2,1,0:T(4,128)S(1)})) conditional(s32[]{:T(128)} %clamp.3, (bf16[4,1024,128]{2,1,0:T(8,128)(2,1)}, bf16[4,1024,128]{2,1,0:T(8,128)(2,1)}, bf16[2,2,8]{2,1,0:T(2,128)(2,1)}, s32[8]{0:T(128)}, s32[1]{0:T(128)}, ...), branch_computations={%region_1.0_spmd, %region_2.0_spmd, %region_3.0_spmd} | conditional | flops 100000000 | bytes 4000008 | solution.py:509
  3.4 67.5 %branch_0_fun.1 = (bf16[4,1216,128]{2,1,0:T(8,128)(2,1)S(1)}, bf16[128,128]{1,0:T(8,128)(2,1)S(1)}, f32[2,4,16]{2,1,0:T(4,128)S(1)}) custom-call(bf16[4,1024,128]{2,1,0:T(8,128)(2,1)} %get-tuple-element.59.kv_hbm, bf16[4,1024,128]{2,1,0:T(8,128)(2,1)} %get-tuple-element.60.codes_hbm, bf16[2,2,8]{2,1,0:T(2,128)(2,1)} %get-tuple-element.61.scales_hbm, ...), custom_call_target="tpu_custom_call" | custom-call | flops 100000000 | bytes 4000000 | tf_op jit(solution)/shard_map/cond/branch_0_fun/pallas_call | solution.py:453
  71.2 1.0 %copy.25 = bf16[2,2,1216,1,128]{4,2,3,1,0:T(8,128)(2,1)} copy(bf16[2,2,1216,1,128]{4,2,3,1,0:T(8,128)(2,1)S(1)} %bitcast.15) | data formatting | bytes 2490368
  72.2 0.6 copy.26
  72.8 0.6 copy.27

commit v6 on v5

--- a/solution.py
+++ b/solution.py
@@ -162,7 +162,7 @@
         s_copy(o).start()
 
     def a_copy(n):
-        rows = slice(n * (CTX // A_PARTS), (n + 1) * (CTX // A_PARTS))
+        rows = pl.ds(pl.multiple_of(n * (CTX // A_PARTS), CTX // A_PARTS), CTX // A_PARTS)
         return pltpu.make_async_remote_copy(
             src_ref=kv.at[:, rows, :], dst_ref=lower.at[:, rows, :], send_sem=a_send, recv_sem=a_recv.at[n],
             device_id=(ring(z + 1), g, k), device_id_type=MESH)
@@ -191,22 +191,28 @@
     alive = z != fc
     CH = 256
 
-    top_own = jnp.full((1, HD), far_below, F32)
-    for n in range(CTX // CH):
-        rows = slice(n * CH, (n + 1) * CH)
+    def rows_of(n, size):
+        return pl.ds(pl.multiple_of(n * size, size), size)
+
+    def score_step(n, top):
+        rows = rows_of(n, CH)
         s = (dot_tt(kv[0, rows, :], q0) + dot_tt(kv[1, rows, :], q1)) * scaling
         s = jnp.where(alive, s, far_below)
         score[rows, :] = s
-        top_own = jnp.maximum(top_own, jnp.max(s, axis=0, keepdims=True))
-    total_own = jnp.zeros((1, HD), F32)
-    for n in range(CTX // CH):
-        rows = slice(n * CH, (n + 1) * CH)
+        return jnp.maximum(top, jnp.max(s, axis=0, keepdims=True))
+
+    top_own = lax.fori_loop(0, CTX // CH, score_step, jnp.full((1, HD), far_below, F32))
+    own_mix[...] = jnp.zeros((HD, HD), F32)
+
+    def weigh_step(n, total):
+        rows = rows_of(n, CH)
         w = jnp.where(alive, jnp.exp(score[rows, :] - top_own), 0.0)
-        total_own = total_own + jnp.sum(w, axis=0, keepdims=True)
         w0 = jnp.where(first_half, w, 0.0).astype(BF16)
         w1 = jnp.where(first_half, 0.0, w).astype(BF16)
-        mix = dot_sum_rows(kv[2, rows, :], w0) + dot_sum_rows(kv[3, rows, :], w1)
-        own_mix[...] = mix if n == 0 else own_mix[...] + mix
+        own_mix[...] += dot_sum_rows(kv[2, rows, :], w0) + dot_sum_rows(kv[3, rows, :], w1)
+        return total + jnp.sum(w, axis=0, keepdims=True)
+
+    total_own = lax.fori_loop(0, CTX // CH, weigh_step, jnp.zeros((1, HD), F32))
     tile = stat_tile(row, top_own, total_own)
     for i in range(N // 2):
         sent_mix[i, :16, :] = own_mix[16 * i:16 * i + 16, :].astype(BF16)
@@ -229,12 +235,15 @@
     shared = (shared ^ (shared >> 1)) & 1
     signs = (1 - 2 * shared).astype(F32).astype(BF16)
 
+    def widen_step(n, carry):
+        for i in range(4):
+            ext[i, pl.ds(pl.multiple_of(CTX + n * PIECE, PIECE), PIECE), :] = kv[i, rows_of(n, PIECE), :].astype(F32)
+        return carry
+
+    lax.fori_loop(0, N, widen_step, 0)
     for i in range(4):
-        for n in range(CTX // CH):
-            ext[i, CTX + n * CH:CTX + (n + 1) * CH, :] = kv[i, n * CH:(n + 1) * CH, :].astype(F32)
         ext[i, 2 * CTX:, :] = jnp.zeros((CAP - CTX, HD), F32)
 
-    whole(bbuf.at[0:N - 1], b_send, b_recv).wait_recv()
     whole(srow.at[0:N - 1], s_send, s_recv).wait_recv()
     away = [ring(z - h) for h in holder]
     away = [jnp.where(v == 0, N - 1, v - 1) for v in away]
@@ -248,6 +257,9 @@
                 at = (2 * p + s) * BLOCKS + b
                 tiles[p] = jnp.where(row == 2 * b + s, line[:, at:at + 1], tiles[p])
 
+    whole(bbuf.at[0:N - 1], b_send, b_recv).wait_recv()
+    a_step(1)
+
     def x_copy(j, p, slot):
         return pltpu.make_async_remote_copy(
             src_ref=xsend.at[p], dst_ref=xbuf.at[p, slot],
@@ -275,7 +287,7 @@
         for o in odd:
             sl_copy(o).start()
 
-    a_step(3)
+    a_step(2)
 
     def one_copy(t, p, piece):
         return pltpu.make_async_remote_copy(
@@ -309,9 +321,7 @@
         up_copy(0, p, z).start()
         one_copy(0, p, z).start()
 
-    lost = {}
-
-    def lost_pieces(pieces):
+    def lost_pieces(pieces, lost):
         count = len(pieces)
         keys = jnp.concatenate([msgs[c, 0] for c in pieces], axis=0)
         values = jnp.concatenate([msgs[c, 1] for c in pieces], axis=0)
@@ -319,29 +329,33 @@
         s = jnp.where(matching, dot_tt(keys, queries) * scaling, far_below)
         top = jnp.max(s, axis=0, keepdims=True)
         if lost:
-            top = jnp.maximum(top, lost["top"])
+            top = jnp.maximum(top, lost[0])
         w = jnp.where(matching, jnp.exp(s - top), 0.0)
         total = jnp.sum(w, axis=0, keepdims=True)
         mix = dot_sum_rows(values, w.astype(BF16))
         if lost:
-            factor = jnp.exp(lost["top"] - top)
-            total = total + lost["total"] * factor
+            factor = jnp.exp(lost[0] - top)
+            total = total + lost[1] * factor
             mix = mix + lost_mix[...] * factor
         lost_mix[...] = mix
-        lost["top"], lost["total"] = top, total
-        for c in pieces:
-            for p in range(2):
-                for b in range(BLOCKS):
-                    tile = msgs[c, p, b * 16:(b + 1) * 16, :].astype(F32)
-                    below = pl.ds(pl.multiple_of(b * BLK + c * SUB, SUB), SUB)
-                    here = pl.ds(pl.multiple_of(CTX + b * BLK + c * SUB, SUB), SUB)
+
+        def place(b, carry):
+            for c in pieces:
+                below = pl.ds(pl.multiple_of(b * BLK + c * SUB, SUB), SUB)
+                here = pl.ds(pl.multiple_of(CTX + b * BLK + c * SUB, SUB), SUB)
+                for p in range(2):
+                    tile = msgs[c, p, rows_of(b, 16), :].astype(F32)
                     for s in range(2):
                         rebuilt = tile[s * SUB:(s + 1) * SUB]
                         ext[2 * p + s, here, :] = jnp.where(z == fc, rebuilt, ext[2 * p + s, here, :])
                         ext[2 * p + s, below, :] = jnp.where(z - 1 == fc, rebuilt, ext[2 * p + s, below, :])
-
-    a_step(2)
-    lost_pieces([z])
+            return carry
+
+        lax.fori_loop(0, BLOCKS, place, 0)
+        return top, total
+
+    a_step(1)
+    first_lost = lost_pieces([z], None)
 
     @pl.when(merging)
     def _():
@@ -358,33 +372,45 @@
 
     lost_below = z - 1 == fc
 
-    def lower_parts(first, last):
+    def lower_part(n):
         @pl.when(z != 0)
         def _():
-            for n in range(first, last):
-                a_copy(n).wait_recv()
-
-        for n in range(first, last):
-            rows = slice(n * (CTX // A_PARTS), (n + 1) * (CTX // A_PARTS))
-            for i in range(4):
-                ext[i, rows, :] = jnp.where(lost_below, ext[i, rows, :], lower[i, rows, :].astype(F32))
-
-    lower_at = {3: (0, 3), 4: (3, 5), 5: (5, 7)}
-    for t in range(1, HOPS + 1):
+            a_copy(n).wait_recv()
+
+        rows = rows_of(n, CTX // A_PARTS)
+        for i in range(4):
+            ext[i, rows, :] = jnp.where(lost_below, ext[i, rows, :], lower[i, rows, :].astype(F32))
+
+    def hop(t, lost):
         for p in range(2):
             two_copy(t - 1, p, ring(z + 2 * t)).wait_recv()
-            if t < HOPS:
+
+            @pl.when(t < HOPS)
+            def _():
                 two_copy(t, p, ring(z + 2 * t)).start()
                 one_copy(t, p, ring(z + 2 * t)).start()
+
+        for p in range(2):
             up_copy(t - 1, p, ring(z - t)).wait_recv()
-            if t < HOPS:
+
+            @pl.when(t < HOPS)
+            def _():
                 up_copy(t, p, ring(z - t)).start()
-        a_step(1)
-        if t in lower_at:
-            lower_parts(*lower_at[t])
+
+        @pl.when((t <= A_PARTS - 4) & (z != N - 1))
+        def _():
+            a_copy(3 + t).start()
+
+        @pl.when(t >= 3)
+        def _():
+            for u in range(2):
+                lower_part(2 * (t - 3) + u)
+
         for p in range(2):
             one_copy(t - 1, p, ring(z + 2 * t - 1)).wait_recv()
-        lost_pieces([ring(z + 2 * t - 1), ring(z + 2 * t), ring(z - t)])
+        return lost_pieces([ring(z + 2 * t - 1), ring(z + 2 * t), ring(z - t)], lost)
+
+    top_lost, total_lost = lax.fori_loop(1, HOPS + 1, hop, first_lost)
     @pl.when(merging)
     def _():
         whole(merged.at[0:N // 2 - 1], me_send, me_recv).wait_recv()
@@ -397,8 +423,8 @@
         all_mix[lax.rem(my_slice + N - n - jnp.where(merging, 1, 0), N // 2)] = merged[n, :16, :].astype(F32)
     top_alive, total_alive = stat_rows(merged[0, 16:, :])
 
-    tops = [top_fresh, lost["top"], top_alive]
-    totals = [total_fresh, lost["total"], total_alive]
+    tops = [top_fresh, top_lost, top_alive]
+    totals = [total_fresh, total_lost, total_alive]
     top = functools.reduce(jnp.maximum, tops)
     factors = [jnp.exp(v - top) for v in tops]
     total = functools.reduce(jnp.add, [v * f for v, f in zip(totals, factors)])
@@ -410,7 +436,9 @@
         turned = log_row if n == 0 else pltpu.roll(log_row, HD - 16 * n, 1)
         logs[n // 4, n % 4:n % 4 + 1, :] = turned[:, :16]
 
-    lower_parts(7, A_PARTS)
+    for n in range(6, A_PARTS):
+        lower_part(n)
+    offsets, filled = [], []
     for seq in range(2):
         begin = jnp.int32(0)
         length = jnp.int32(0)
@@ -418,13 +446,19 @@
             size = lengths[seq, j]
             begin = begin + jnp.where(j < z - 1, size, 0)
             length = jnp.where(j == z - 1, size, length)
-        offset = jnp.clip(begin - (z - 1) * CTX, 0, CTX)
-        slot = iota((PIECE, HD), 0)
+        offsets.append(jnp.clip(begin - (z - 1) * CTX, 0, CTX))
+        filled.append(length)
+    slot = iota((PIECE, HD), 0)
+
+    def final_step(n, carry):
         for p in range(2):
-            for n in range(CAP // PIECE):
-                rows = ext[2 * p + seq, pl.ds(offset + n * PIECE, PIECE), :]
-                rows = jnp.where(slot + n * PIECE < length, rows, 0.0)
-                out[2 * p + seq, n * PIECE:(n + 1) * PIECE, :] = rows.astype(BF16)
+            for seq in range(2):
+                rows = ext[2 * p + seq, pl.ds(offsets[seq] + n * PIECE, PIECE), :]
+                rows = jnp.where(slot < filled[seq] - n * PIECE, rows, 0.0)
+                out[2 * p + seq, rows_of(n, PIECE), :] = rows.astype(BF16)
+        return carry
+
+    lax.fori_loop(0, CAP // PIECE, final_step, 0)
 
     whole(bbuf.at[0:N - 1], b_send, b_recv).wait_send()
     whole(srow.at[0:N - 1], s_send, s_recv).wait_send()
@@ -500,12 +534,13 @@
 
 
 def body(kv_cache, backup_codes, backup_scales, block_shift, failed, new_lengths, queries, new_kv):
-    cube = (BLOCKS,) * 3
-    ids = [lax.broadcasted_iota(jnp.int32, cube, n) for n in range(3)]
-    spread = [lax.broadcast_in_dim(block_shift, cube, (n,)) for n in range(3)]
-    equal = (spread[0] == spread[1]) & (spread[1] == spread[2]) & (ids[0] < ids[1]) & (ids[1] < ids[2])
-    triples = jnp.sum(equal.astype(jnp.int32))
-    branch = (triples > 0).astype(jnp.int32) + (triples > 3).astype(jnp.int32)
+    tens = jnp.uint32(1) << (4 * (block_shift & 7)).astype(jnp.uint32)
+    low = jnp.sum(jnp.where(block_shift < 8, tens, 0), dtype=jnp.uint32)
+    high = jnp.sum(jnp.where(block_shift < 8, 0, tens), dtype=jnp.uint32)
+    tops = jnp.uint32(0x88888888)
+    three = ((low + jnp.uint32(0x55555555)) | (high + jnp.uint32(0x55555555))) & tops
+    four = ((low + jnp.uint32(0x44444444)) | (high + jnp.uint32(0x44444444))) & tops
+    branch = (three != 0).astype(jnp.int32) + (four != 0).astype(jnp.int32)
     out, att, logs = lax.switch(
         branch,
         [functools.partial(restore, slots) for slots in SLOTS],

time: 74.6 us -> 72.6 us (0.973)
  Pallas kernels: 67.5 us -> 64.9 us
  between operations: 1.94 us -> 3.24 us
    pallas_call x1, Pallas kernels: 67.5 us -> 64.9 us  [restore(): pl.pallas_call(functools.partial(kernel, slots), out_shape=(jax.ShapeDtyp...]
where the time goes in v6:
time: 72.6 us; the launch traced here: 71.7 us
  Pallas kernels  64.9 us (89%)
  between operations  3.24 us (4%)
  local copies, waits for them, and re-layouts  2.24 us (3%)
  other arithmetic  1.3 us (2%)
    pallas_call x1, Pallas kernels, restore(): pl.pallas_call(functools.partial(kernel, slots), out_shape=(jax.ShapeDtyp...  64.9 us
    unnamed x3, local copies, waits for them, and re-layouts  2.24 us

profile of v6, /device:TPU:6, one launch (start us, length us, event | category | flops | bytes accessed | tf_op | source)
XLA Modules:
  0.0 71.7 jit_solution(10162876827581479710)
XLA Ops:
  0.6 1.3 %fusion.1 = (u32[]{:T(128)}, u32[]{:T(128)}) fusion(s32[8]{0:T(128)} %param.14), kind=kLoop, calls=%fused_computation.3 | loop fusion | flops 70 | bytes 40 | tf_op jit(solution)/shard_map/reduce_sum | solution.py:539
  4.5 64.9 %conditional.1 = ((bf16[4,1216,128]{2,1,0:T(8,128)(2,1)S(1)}, bf16[128,128]{1,0:T(8,128)(2,1)S(1)}, f32[2,4,16]{2,1,0:T(4,128)S(1)})) conditional(s32[]{:T(128)} %clamp.3, (bf16[4,1024,128]{2,1,0:T(8,128)(2,1)}, bf16[4,1024,128]{2,1,0:T(8,128)(2,1)}, bf16[2,2,8]{2,1,0:T(2,128)(2,1)}, s32[8]{0:T(128)}, s32[1]{0:T(128)}, ...), branch_computations={%region_2.3_spmd, %region_3.4_spmd, %region_4.5_spmd} | conditional | flops 100000000 | bytes 4000008 | solution.py:544
  4.5 64.9 %branch_0_fun.1 = (bf16[4,1216,128]{2,1,0:T(8,128)(2,1)S(1)}, bf16[128,128]{1,0:T(8,128)(2,1)S(1)}, f32[2,4,16]{2,1,0:T(4,128)S(1)}) custom-call(bf16[4,1024,128]{2,1,0:T(8,128)(2,1)} %get-tuple-element.59.kv_hbm, bf16[4,1024,128]{2,1,0:T(8,128)(2,1)} %get-tuple-element.60.codes_hbm, bf16[2,2,8]{2,1,0:T(2,128)(2,1)} %get-tuple-element.61.scales_hbm, ...), custom_call_target="tpu_custom_call" | custom-call | flops 100000000 | bytes 4000000 | tf_op jit(solution)/shard_map/cond/branch_0_fun/pallas_call | solution.py:487
  69.5 1.0 %copy.24 = bf16[2,2,1216,1,128]{4,2,3,1,0:T(8,128)(2,1)} copy(bf16[2,2,1216,1,128]{4,2,3,1,0:T(8,128)(2,1)S(1)} %bitcast.15) | data formatting | bytes 2490368
  70.5 0.6 copy.25
  71.1 0.6 copy.26
